TPU v7x, 512 devices: a whole 4x4x16 slice. The times are simulated.
512 devices in a mesh: section: 8 (over y, x_hi), seq: 64 (over x_lo, z, core).
Axes of the slice: x: 4 (x_hi: 2, x_lo: 2; x = x_hi * 2 + x_lo), y: 4, z: 16, core: 2. Of those that a mesh axis runs over, the one named last changes fastest.
Arguments:
- sent_codes: bfloat16 [8, 8192, 512], P('section', 'seq'), may hold values from -6 to 6
- start_codes: bfloat16 [8192, 512], P('seq'), may hold values from -6 to 6
- sent_grads: bfloat16 [8, 8192, 512], P('section', 'seq'), may hold values from -6 to 6
- loss_grads: bfloat16 [8192, 512], P('seq'), may hold values from -6 to 6
- w_query: bfloat16 [8, 512, 512], P('section'), may hold values from -0.25 to 0.25
- w_key: bfloat16 [8, 512, 128], P('section'), may hold values from -0.25 to 0.25
- w_value: bfloat16 [8, 512, 128], P('section'), may hold values from -0.078125 to 0.078125
- w_out: bfloat16 [8, 512, 512], P('section'), may hold values from -0.75 to 0.75
- q_gain: float32 [8, 128], P('section'), may hold values from 0.8 to 5.5, as said below
- k_gain: float32 [8, 128], P('section'), may hold values from 0.8 to 5.5, as said below
Outputs:
- out_codes: bfloat16 [8, 8192, 512], P('section', 'seq')
- in_grads: bfloat16 [8, 8192, 512], P('section', 'seq')
Inputs may be any that keep to these rules, and one draw needn't show every extreme that they name: `q_gain`: positive per-channel gains, one row per section. `k_gain`: positive per-channel gains, one row per section.
All inputs are finite; a program needn't handle non-finite values.
Results may differ from a plain program's by a relative error of at most 0.035.
The roundings to bfloat16 on the way count: a program that leaves them out, or rounds other values in their place, can miss the bound.
Values may be sent and summed in bfloat16 or wider, within the bound.
A program may use at most 64 MiB of HBM per device.

v0:
```python
import jax
import jax.numpy as jnp
from jax import lax
from jax.sharding import PartitionSpec as P

D = 5120


ROPE_BASE = 1000000.0
NORM_EPS = 1e-06
MASK_FILL = -1e30


def from_behind(block, axis, distance):
    devices = range(lax.axis_size(axis))
    route = [(i - distance, i) for i in devices if i - distance in devices]
    return lax.ppermute(block, axis, route)


def rotate_half(tensor):
    half_dim = tensor.shape[-1] // 2
    return jnp.concatenate([-tensor[..., half_dim:], tensor[..., :half_dim]], axis=-1)


def rotate_back(tensor):
    half_dim = tensor.shape[-1] // 2
    return jnp.concatenate([tensor[..., half_dim:], -tensor[..., :half_dim]], axis=-1)


def rope_tables(positions, head_dim):
    half_dim = head_dim // 2
    exponent = jnp.arange(half_dim).astype(jnp.float32) * (2.0 / head_dim)
    frequency = jnp.power(jnp.float32(ROPE_BASE), -exponent)
    angles = positions.astype(jnp.float32)[:, None] * frequency[None, :]
    angles = jnp.concatenate([angles, angles], axis=-1)
    return (jnp.cos(angles), jnp.sin(angles))


def head_norm(tensor, gain_vec):
    inv_rms = lax.rsqrt(jnp.mean(tensor * tensor, axis=-1, keepdims=True) + NORM_EPS)
    return (tensor * inv_rms * gain_vec, inv_rms)


def norm_back(tensor, inv_rms, gain_vec, upstream):
    scaled = upstream * gain_vec
    return inv_rms * scaled - tensor * inv_rms**3 * jnp.mean(
        tensor * scaled, axis=-1, keepdims=True
    )


def project_in(in_codes, query_w, key_w, value_w, query_gain, key_gain, cosines, sines):
    widened = in_codes.astype(jnp.float32)
    inv_norm = lax.rsqrt(jnp.sum(widened * widened, axis=-1, keepdims=True) / D + NORM_EPS)
    normed = (widened * inv_norm).astype(jnp.bfloat16)
    token_count = in_codes.shape[0]
    head_dim = key_w.shape[1]
    query_lin = jnp.dot(normed, query_w, preferred_element_type=jnp.float32).reshape(
        token_count, -1, head_dim
    )
    key_lin = jnp.dot(normed, key_w, preferred_element_type=jnp.float32)
    values = jnp.dot(normed, value_w, preferred_element_type=jnp.float32).astype(jnp.bfloat16)
    query_hat, query_inv = head_norm(query_lin, query_gain)
    key_hat, key_inv = head_norm(key_lin, key_gain)
    query_rot = (
        query_hat * cosines[:, None, :] + rotate_half(query_hat) * sines[:, None, :]
    ).astype(jnp.bfloat16)
    key_rot = (key_hat * cosines + rotate_half(key_hat) * sines).astype(jnp.bfloat16)
    kept_state = (widened, inv_norm, query_lin, query_inv, key_lin, key_inv)
    return (kept_state, query_rot, key_rot, values)


def project_back(
    kept_state,
    grad_codes,
    query_w,
    key_w,
    value_w,
    query_gain,
    key_gain,
    cosines,
    sines,
    query_rot_grad,
    key_rot_grad,
    value_grad,
):
    widened, inv_norm, query_lin, query_inv, key_lin, key_inv = kept_state
    token_count = widened.shape[0]
    query_hat_grad = query_rot_grad * cosines[:, None, :] + rotate_back(
        query_rot_grad * sines[:, None, :]
    )
    key_hat_grad = key_rot_grad * cosines + rotate_back(key_rot_grad * sines)
    query_lin_grad = (
        norm_back(query_lin, query_inv, query_gain, query_hat_grad)
        .reshape(token_count, -1)
        .astype(jnp.bfloat16)
    )
    key_lin_grad = norm_back(key_lin, key_inv, key_gain, key_hat_grad).astype(jnp.bfloat16)
    value_lin_grad = value_grad.astype(jnp.bfloat16)
    normed_grad = jnp.dot(query_lin_grad, query_w.T, preferred_element_type=jnp.float32)
    normed_grad = normed_grad + jnp.dot(key_lin_grad, key_w.T, preferred_element_type=jnp.float32)
    normed_grad = normed_grad + jnp.dot(
        value_lin_grad, value_w.T, preferred_element_type=jnp.float32
    )
    inner_sum = jnp.sum(widened * normed_grad, axis=-1, keepdims=True)
    result = (
        grad_codes.astype(jnp.float32)
        + inv_norm * normed_grad
        - widened * inv_norm**3 * inner_sum / D
    )
    return result.astype(jnp.bfloat16)


def local(
    sent_codes, start_codes, sent_grads, loss_grads, w_query, w_key, w_value, w_out, q_gain, k_gain
):
    section_id = lax.axis_index("section")
    section_total = lax.axis_size("section")
    arrived_codes = from_behind(sent_codes, "section", 1)
    arrived_grads = from_behind(sent_grads, "section", -1)
    in_codes = jnp.where(section_id == 0, start_codes, arrived_codes[0])
    grad_codes = jnp.where(section_id == section_total - 1, loss_grads, arrived_grads[0])
    query_w = w_query[0]
    key_w = w_key[0]
    value_w = w_value[0]
    out_w = w_out[0]
    tokens = in_codes.shape[0]
    head_dim = key_w.shape[1]
    head_count = query_w.shape[1] // head_dim
    row_count = tokens * head_count
    seq_devices = lax.axis_size("seq")
    seq_total = tokens * seq_devices
    first_pos = lax.axis_index("seq") * tokens
    positions = first_pos + jnp.arange(tokens, dtype=jnp.int32)
    cosines, sines = rope_tables(positions, head_dim)
    kept_state, query_rot, key_rot, values = project_in(
        in_codes, query_w, key_w, value_w, q_gain[0], k_gain[0], cosines, sines
    )
    query_flat = query_rot.reshape(row_count, head_dim)
    query_pos = first_pos + jnp.arange(row_count, dtype=jnp.int32) // head_count
    last_pos = first_pos + tokens - 1
    score_scale = head_dim ** (-0.5)
    key_rows = jnp.concatenate([key_rot, values], axis=1)
    key_block = min(seq_total, max(512, tokens))
    contract_last = (((1,), (1,)), ((), ()))
    contract_first = (((0,), (0,)), ((), ()))

    def scores_for(piece, start):
        piece_rows = piece.shape[0]
        key_pos = start + jnp.arange(piece_rows, dtype=jnp.int32)
        visible = key_pos[None, :] <= query_pos[:, None]
        logits = (
            lax.dot_general(
                query_flat, piece[:, :head_dim], contract_last, preferred_element_type=jnp.float32
            )
            * score_scale
        )
        return (logits, visible)

    def in_blocks(step_fn, current, piece):
        piece_rows = piece.shape[0]

        def inner_step(block_index, inner_state):
            sub_piece = lax.dynamic_slice_in_dim(piece, block_index * key_block, key_block, 0)
            return step_fn(inner_state, sub_piece, block_index * key_block)

        return lax.fori_loop(0, piece_rows // key_block, inner_step, current)

    def forward_step(current, piece, start):

        def forward_work(state_now):
            top_old, total_old, summed_old = state_now
            logits, visible = scores_for(piece, start)
            top_new = jnp.maximum(top_old, jnp.max(jnp.where(visible, logits, MASK_FILL), axis=1))
            weights = jnp.where(visible, jnp.exp(logits - top_new[:, None]), 0.0)
            shrink = jnp.exp(top_old - top_new)
            total_new = total_old * shrink + jnp.sum(weights, axis=1)
            summed_new = summed_old * shrink[:, None] + jnp.dot(
                weights.astype(jnp.bfloat16),
                piece[:, head_dim:],
                preferred_element_type=jnp.float32,
            )
            return (top_new, total_new, summed_new)

        return lax.cond(start <= last_pos, forward_work, lambda state_now: state_now, current)

    start_forward = (
        jnp.full((row_count,), MASK_FILL, jnp.float32),
        jnp.zeros((row_count,), jnp.float32),
        jnp.zeros((row_count, head_dim), jnp.float32),
    )
    row_top, row_total, summed = in_blocks(
        forward_step, start_forward, lax.all_gather(key_rows, "seq", axis=0, tiled=True)
    )
    attended = (summed / row_total[:, None]).astype(jnp.bfloat16)
    out_codes = (
        in_codes.astype(jnp.float32)
        + jnp.dot(
            attended.reshape(tokens, head_count * head_dim),
            out_w,
            preferred_element_type=jnp.float32,
        )
    ).astype(jnp.bfloat16)
    grad_att = (
        jnp.dot(grad_codes, out_w.T, preferred_element_type=jnp.float32)
        .astype(jnp.bfloat16)
        .reshape(row_count, head_dim)
    )
    delta_rows = jnp.sum(grad_att.astype(jnp.float32) * attended.astype(jnp.float32), axis=1)

    def backward_step(current, piece, start):

        def backward_work(state_now):
            query_acc, key_part = state_now
            logits, visible = scores_for(piece, start)
            probs = jnp.where(visible, jnp.exp(logits - row_top[:, None]) / row_total[:, None], 0.0)
            grad_prob = lax.dot_general(
                grad_att, piece[:, head_dim:], contract_last, preferred_element_type=jnp.float32
            )
            grad_score = (probs * (grad_prob - delta_rows[:, None]) * score_scale).astype(
                jnp.bfloat16
            )
            query_acc = query_acc + jnp.dot(
                grad_score, piece[:, :head_dim], preferred_element_type=jnp.float32
            )
            key_grad = lax.dot_general(
                grad_score, query_flat, contract_first, preferred_element_type=jnp.float32
            )
            value_grad = lax.dot_general(
                probs.astype(jnp.bfloat16),
                grad_att,
                contract_first,
                preferred_element_type=jnp.float32,
            )
            key_part = lax.dynamic_update_slice_in_dim(
                key_part, jnp.concatenate([key_grad, value_grad], axis=1), start, 0
            )
            return (query_acc, key_part)

        return lax.cond(start <= last_pos, backward_work, lambda state_now: state_now, current)

    start_backward = (
        jnp.zeros((row_count, head_dim), jnp.float32),
        jnp.zeros((seq_total, 2 * head_dim), jnp.float32),
    )
    query_acc, key_part = in_blocks(
        backward_step, start_backward, lax.all_gather(key_rows, "seq", axis=0, tiled=True)
    )
    received = lax.all_to_all(
        key_part.reshape(seq_total, 1, 2 * head_dim), "seq", split_axis=0, concat_axis=1, tiled=True
    )
    kv_grads = jnp.sum(received, axis=1)
    in_grads = project_back(
        kept_state,
        grad_codes,
        query_w,
        key_w,
        value_w,
        q_gain[0],
        k_gain[0],
        cosines,
        sines,
        query_acc.reshape(tokens, head_count, head_dim),
        kv_grads[:, :head_dim],
        kv_grads[:, head_dim:],
    )
    return (out_codes[None], in_grads[None])


def solution(mesh):
    in_specs = (
        P("section", "seq", None),
        P("seq", None),
        P("section", "seq", None),
        P("seq", None),
        P("section", None, None),
        P("section", None, None),
        P("section", None, None),
        P("section", None, None),
        P("section", None),
        P("section", None),
    )
    out_specs = (P("section", "seq", None), P("section", "seq", None))
    return jax.shard_map(local, mesh=mesh, in_specs=in_specs, out_specs=out_specs, check_vma=False)
```

profile of v0, /device:TPU:6, one launch (start us, length us, event | category | flops | bytes accessed | tf_op | source)
XLA Modules:
  0.0 708.8 jit_solution(12115639615640713376)
XLA Ops:
  7.2 4.5 collective-permute-start
  11.8 4.4 collective-permute-done
  24.8 5.7 collective-permute-done.1
  31.7 122.0 %all-gather.2.cloned.1.call-done = bf16[8192,256]{0,1:T(8,128)(2,1)} async-done(((bf16[128,256]{0,1:T(8,128)(2,1)}), bf16[8192,256]{0,1:T(8,128)(2,1)}) %all-gather.2.cloned.1.call-update) | async-done | bytes 4194320 | tf_op jit(solution)/shard_map/all_gather | solution.py:192
  153.7 6.4 copy.34
  160.1 28.0 %while.34 = (s32[]{:T(128)}, f32[512]{0:T(512)S(1)}, f32[512]{0:T(512)S(1)}, f32[512,128]{1,0:T(8,128)S(1)}, s32[]{:T(128)}, /*index=5*/bf16[8192,256]{1,0:T(8,1...) while((s32[]{:T(128)}, f32[512]{0:T(512)S(1)}, f32[512]{0:T(512)S(1)}, ...), condition=%wide.region_8.9_spmd.clone, body=%wide.region_3.8_spmd.clone.sunk | while | flops 137500672 | bytes 4125029 | solution.py:166
  160.2 3.0 conditional.6
  166.3 3.0 conditional.6
  188.4 4.2 broadcast_in_dim.56
  192.6 48.4 %while.35 = (s32[]{:T(128)}, f32[512,128]{1,0:T(8,128)S(1)}, f32[8192,256]{0,1:T(8,128)}, s32[]{:T(128)}, bf16[8192,256]{1,0:T(8,128)(2,1)}, /*index=5*/bf16[512...) while((s32[]{:T(128)}, f32[512,128]{1,0:T(8,128)S(1)}, ...), condition=%wide.region_13.14_spmd.clone, body=%wide.region_10.13_spmd.clone.sunk | while | flops 338367488 | bytes 7760269 | solution.py:166
  192.6 5.3 conditional.7
  197.9 5.3 conditional.7
  203.3 5.3 conditional.7
  208.6 5.3 conditional.7
  213.9 5.3 conditional.7
  219.2 5.3 conditional.7
  224.5 5.3 conditional.7
  229.9 5.4 conditional.7
  235.3 5.3 conditional.7
  241.0 18.1 %copy.41 = f32[8192,1,256]{2,1,0:T(1,128)} copy(f32[8192,1,256]{0,2,1:T(8,128)} %bitcast.76) | data formatting | bytes 16777216 | tf_op jit(solution)/shard_map/reshape | solution.py:249
  259.1 63.8 %all-to-all-start = ((f32[8192,1,256]{2,1,0:T(1,128)}), f32[8192,1,256]{2,1,0:T(1,128)}, u32[]{:S(2)}, u32[]{:S(2)}) async-start(f32[8192,1,256]{2,1,0:T(1,128)} %copy.41), calls=%async_computation | async-start | bytes 16777216 | tf_op jit(solution)/shard_map/all_to_all | solution.py:248
  324.6 364.1 %all-to-all-done = f32[8192,1,256]{2,1,0:T(1,128)} async-done(((f32[8192,1,256]{2,1,0:T(1,128)}), f32[8192,1,256]{2,1,0:T(1,128)}, u32[]{:S(2)}, u32[]{:S(2)}) %all-to-all-start) | async-done | bytes 8388640 | tf_op jit(solution)/shard_map/all_to_all | solution.py:248
  688.7 7.2 %copy.43 = f32[8192,1,256]{2,0,1:T(8,128)} copy(f32[8192,1,256]{2,1,0:T(1,128)} %all-to-all-done) | data formatting | bytes 16777216
  695.8 3.9 reduce_sum.88
  (272 shorter events, 109.4 us)
Async XLA Ops:
  7.2 23.4 %copy-start = (bf16[1,512,512]{2,1,0:T(8,128)(2,1)S(1)}, bf16[1,512,512]{2,1,0:T(8,128)(2,1)}, u32[]{:S(2)}) copy-start(bf16[1,512,512]{2,1,0:T(8,128)(2,1)} %param.25) | copy-start | bytes 1572868
  7.2 24.2 %copy-start.6 = (f32[1,128]{1,0:T(1,128)S(1)}, f32[1,128]{1,0:T(1,128)}, u32[]{:S(2)}) copy-start(f32[1,128]{1,0:T(1,128)} %param.26) | copy-start | bytes 1540
  7.2 146.5 %all-gather.2.cloned.1.call-start = ((), (), s32[]{:S(2)}) async-start(), calls=%async_computation.1 | async-start | bytes 4259840 | tf_op jit(solution)/shard_map/all_gather | solution.py:192
  7.2 9.0 %collective-permute-start = (bf16[1,128,512]{2,1,0:T(8,128)(2,1)}, bf16[1,128,512]{2,1,0:T(8,128)(2,1)S(1)}, u32[]{:S(2)}, u32[]{:S(2)}) collective-permute-start(bf16[1,128,512]{2,1,0:T(8,128)(2,1)} %param.18), channel_id=1, source_target_pairs={{0,64},{64,128},{128,192},{192,256},{256,320},{320,384},{384,448},... | collective-permute-start | bytes 393224 | tf_op jit(solution)/shard_map/ppermute | solution.py:17
  21.1 9.5 %collective-permute-start.1 = (bf16[1,128,512]{2,1,0:T(8,128)(2,1)}, bf16[1,128,512]{2,1,0:T(8,128)(2,1)S(1)}, u32[]{:S(2)}, u32[]{:S(2)}) collective-permute-start(bf16[1,128,512]{2,1,0:T(8,128)(2,1)} %param.20), channel_id=1, source_target_pairs={{64,0},{128,64},{192,128},{256,192},{320,256},{384,320},{448,384},... | collective-permute-start | bytes 393224 | tf_op jit(solution)/shard_map/ppermute | solution.py:17
  259.1 429.6 %all-to-all-start = ((f32[8192,1,256]{2,1,0:T(1,128)}), f32[8192,1,256]{2,1,0:T(1,128)}, u32[]{:S(2)}, u32[]{:S(2)}) async-start(f32[8192,1,256]{2,1,0:T(1,128)} %copy.41), calls=%async_computation | async-start | bytes 16777216 | tf_op jit(solution)/shard_map/all_to_all | solution.py:248
  322.9 1.4 copy-start.1
  695.8 4.3 copy-start.5
  695.8 4.6 copy-start.2
  695.8 5.0 copy-start.4
  695.8 5.3 copy-start.3
Sparse Core Ops, SparseCore 0:
  21.2 132.4 all-gather.1
where the time goes:
time: 711 us; the launch traced here: 709 us
  waiting for transfers between devices  496 us (70%)
  starting transfers between devices  70.7 us (10%)
  matrix products  68.8 us (10%)
  local copies, waits for them, and re-layouts  37.8 us (5%)
  other arithmetic  18.9 us (3%)
  between operations  14.3 us (2%)
    all_to_all x1, waiting for transfers between devices, local(): lax.all_to_all(key_part.reshape(seq_total, 1, 2 * head_dim), 'seq', split...  364 us
    all_gather x1, waiting for transfers between devices, local(): lax.all_gather(key_rows, 'seq', axis=0, tiled=True)  122 us
    all_to_all x1, starting transfers between devices, local(): lax.all_to_all(key_part.reshape(seq_total, 1, 2 * head_dim), 'seq', split...  63.8 us
    dot_general x18, matrix products, scores_for(): lax.dot_general(query_flat, piece[:, :head_dim], contract_last, preferred...  22.9 us
    reshape x1, local copies, waits for them, and re-layouts, local(): key_part.reshape(seq_total, 1, 2 * head_dim)  18.1 us
  transfers between devices with their start and end apart: 4, of which 4 were waited for; matrix products, arithmetic and copies ran while one was open for 1% of the time, Pallas kernels for 0%

commit v1 on v0

v1 whole, which is shorter than its diff:
```python
import functools

import jax
import jax.numpy as jnp
from jax import lax
from jax.experimental import pallas as pl
from jax.experimental.pallas import tpu as pltpu
from jax.sharding import PartitionSpec as P

D = 5120
ROPE_BASE = 1000000.0
NORM_EPS = 1e-06
MASK_FILL = -1e30
LOG2_E = 1.4426950408889634
MESH = pl.DeviceIdType.MESH
F32 = jnp.float32
BF16 = jnp.bfloat16
TOK = 128
HD = 128
CONTRACT_LAST = (((1,), (1,)), ((), ()))
CONTRACT_FIRST = (((0,), (0,)), ((), ()))

CODES, GRADS, KV_X, Q_X, DO_X, ATT_X, DQ_X, DKV_X = range(8)


def dot(a, b):
    return jnp.dot(a, b, preferred_element_type=F32)


def dot_last(a, b):
    return lax.dot_general(a, b, CONTRACT_LAST, preferred_element_type=F32)


def dot_first(a, b):
    return lax.dot_general(a, b, CONTRACT_FIRST, preferred_element_type=F32)


def rows(start, count=TOK):
    return pl.ds(pl.multiple_of(start, TOK), count)


def kernel(
    ring,
    sections,
    sent_codes,
    start_codes,
    sent_grads,
    loss_grads,
    w_query,
    w_key,
    w_value,
    w_out,
    q_gain,
    k_gain,
    cosines,
    sines,
    out_codes,
    in_grads,
    codes_buf,
    grads_buf,
    codes_in,
    grads_in,
    q_lin,
    k_lin,
    q_own,
    q_rows,
    q_cols,
    do_own,
    do_rows,
    do_cols,
    kv,
    top,
    total,
    acc,
    delta,
    att_rows,
    att_own,
    dq_cols,
    dq_rows,
    dq_own,
    part,
    part_core,
    ring_out,
    ring_in,
    kv_total,
    kv_peer,
    once_send,
    once_recv,
    gather_send,
    gather_recv,
    core_send,
    core_recv,
    reduce_send,
    reduce_recv,
    swap_send,
    swap_recv,
):
    half = ring // 2
    sec = lax.axis_index("section")
    me = lax.axis_index("seq")
    x = lax.div(me, 2 * ring)
    z = lax.rem(lax.div(me, 2), ring)
    c = lax.rem(me, 2)

    def device(xx, zz, cc):
        return (sec, (xx * ring + zz) * 2 + cc)

    along = (device(x, lax.rem(z + 1, ring), c), device(x, lax.rem(z + ring - 1, ring), c))
    other_core = device(x, z, 1 - c)
    across = device(1 - x, z, c)
    next_section = (lax.rem(sec + 1, sections), me)
    last_section = (lax.rem(sec + sections - 1, sections), me)

    def copy(src, dst, send, recv, target):
        return pltpu.make_async_remote_copy(
            src_ref=src,
            dst_ref=dst,
            send_sem=send,
            recv_sem=recv,
            device_id=target,
            device_id_type=MESH,
        )

    def copy_once(number, src, dst, target):
        return copy(src, dst, once_send.at[number], once_recv.at[number], target)

    barrier = pltpu.get_barrier_semaphore()
    for partner in (along[0], along[1], other_core, across, next_section, last_section):
        pl.semaphore_signal(barrier, inc=1, device_id=partner, device_id_type=MESH)
    pl.semaphore_wait(barrier, 6)

    codes_copy = copy_once(CODES, sent_codes, codes_buf, next_section)
    grads_copy = copy_once(GRADS, sent_grads, grads_buf, last_section)
    codes_copy.start()
    grads_copy.start()

    top[...] = jnp.full(top.shape, MASK_FILL, F32)
    total[...] = jnp.zeros(total.shape, F32)
    acc[...] = jnp.zeros(acc.shape, F32)
    dq_cols[...] = jnp.zeros(dq_cols.shape, F32)
    for way, farthest in ((0, half), (1, half - 1)):
        ring_in[way, farthest] = jnp.zeros(ring_in.shape[2:], BF16)

    lane = lax.broadcasted_iota(jnp.int32, (TOK, HD), 1)
    first_half = lane < HD // 2
    cos = cosines[...]
    sin = sines[...]
    sin_turned = jnp.where(first_half, -sin, sin)

    def head_norm(tensor, gain):
        inv = lax.rsqrt(jnp.mean(tensor * tensor, axis=-1, keepdims=True) + NORM_EPS)
        hat = tensor * inv * gain
        return (hat * cos + pltpu.roll(hat, HD // 2, 1) * sin_turned).astype(BF16)

    def norm_back(tensor, gain, rot_grad):
        turned = pltpu.roll(rot_grad * sin, HD // 2, 1)
        hat_grad = rot_grad * cos + jnp.where(first_half, turned, -turned)
        inv = lax.rsqrt(jnp.mean(tensor * tensor, axis=-1, keepdims=True) + NORM_EPS)
        scaled = hat_grad * gain
        inner = jnp.mean(tensor * scaled, axis=-1, keepdims=True)
        return (inv * scaled - tensor * (inv * inv * inv) * inner).astype(BF16)

    def chunk(zz, xx, cc):
        return kv.at[rows(((zz * 2 + xx) * 2 + cc) * TOK)]

    def place(way, step):
        return lax.rem(z + (ring - step if way == 0 else step), ring)

    def group_x(group):
        return x if group == 0 else 1 - x

    def gather_copy(way, step, group, zz):
        ref = chunk(zz, group_x(group), c)
        sems = (gather_send.at[way, step, group], gather_recv.at[way, step, group])
        return copy(ref, ref, *sems, along[way])

    def core_copy(way, step, group, zz, cc):
        ref = chunk(zz, group_x(group), cc)
        sems = (core_send.at[way, step, group], core_recv.at[way, step, group])
        return copy(ref, ref, *sems, other_core)

    codes_copy.wait_recv()

    @pl.when(sec == 0)
    def _():
        codes_in[...] = start_codes[...]

    @pl.when(sec != 0)
    def _():
        codes_in[...] = codes_buf[...]

    wide = codes_in[...].astype(F32)
    inv_norm = lax.rsqrt(jnp.sum(wide * wide, axis=-1, keepdims=True) / D + NORM_EPS)
    normed = (wide * inv_norm).astype(BF16)
    key_lin = dot(normed, w_key[...])
    k_lin[...] = key_lin
    own = rows(((z * 2 + x) * 2 + c) * TOK)
    kv[own, :HD] = head_norm(key_lin, k_gain[...])
    kv[own, HD:] = dot(normed, w_value[...]).astype(BF16)

    kv_copy = copy_once(KV_X, chunk(z, x, c), chunk(z, x, c), across)
    kv_copy.start()
    for way in range(2):
        gather_copy(way, 1, 0, z).start()
    core_copy(0, 0, 0, z, c).start()

    q_lin[...] = dot(normed, w_query[...])
    for head in range(4):
        q_own[head * TOK : (head + 1) * TOK, :] = head_norm(
            q_lin[:, head * HD : (head + 1) * HD], q_gain[...]
        )
    peer_heads = rows((1 - x) * 2 * TOK, 2 * TOK)
    own_heads = rows(x * 2 * TOK, 2 * TOK)
    q_copy = copy_once(Q_X, q_own.at[peer_heads], q_rows.at[own_heads], across)
    q_copy.start()
    q_rows[own_heads, :] = q_own[own_heads, :]

    kv_copy.wait_recv()
    for way in range(2):
        gather_copy(way, 1, 1, z).start()
    core_copy(0, 0, 1, z, c).start()

    grads_copy.wait_recv()

    @pl.when(sec == sections - 1)
    def _():
        grads_in[...] = loss_grads[...]

    @pl.when(sec != sections - 1)
    def _():
        grads_in[...] = grads_buf[...]

    grad_att = dot_last(grads_in[...], w_out[...]).astype(BF16)
    for head in range(4):
        do_own[head * TOK : (head + 1) * TOK, :] = grad_att[:, head * HD : (head + 1) * HD]
    do_copy = copy_once(DO_X, do_own.at[peer_heads], do_rows.at[own_heads], across)
    do_copy.start()
    do_rows[own_heads, :] = do_own[own_heads, :]

    def turn(src, dst):
        for block in range(4):
            span = slice(block * TOK, (block + 1) * TOK)
            dst[:, span] = src[span, :].T

    q_copy.wait_recv()
    turn(q_rows, q_cols)

    scale = HD ** (-0.5)
    scale_two = scale * LOG2_E

    def own_mask(first_col):
        key = lax.broadcasted_iota(jnp.int32, (2 * TOK, 4 * TOK - first_col), 0)
        col = lax.broadcasted_iota(jnp.int32, (2 * TOK, 4 * TOK - first_col), 1) + first_col
        query = lax.rem(col, TOK) + c * TOK
        visible = key <= query
        if first_col == 0:
            visible = visible | (col >= 2 * TOK)
        return visible

    def forward_tile(start, first_col, masked):
        span = slice(first_col, 4 * TOK)
        block = rows(start, 2 * TOK)
        scores = dot(kv[block, :HD], q_cols[:, span]) * scale_two
        if masked:
            scores = jnp.where(own_mask(first_col), scores, 2 * MASK_FILL)
        top_old = top[:, span]
        top_new = jnp.maximum(top_old, jnp.max(scores, axis=0, keepdims=True))
        weights = jnp.exp2(scores - top_new)
        shrink = jnp.exp2(top_old - top_new)
        total[:, span] = total[:, span] * shrink + jnp.sum(weights, axis=0, keepdims=True)
        acc[:, span] = acc[:, span] * shrink + dot_first(kv[block, HD:], weights.astype(BF16))
        top[:, span] = top_new

    def arrive(way, step, forward):
        zz = place(way, step)
        for group in range(2):
            gather_copy(way, step, group, zz).wait_recv()

            @pl.when(forward)
            def _():
                gather_copy(way, step + 1, group, zz).start()

            core_copy(way, step, group, zz, c).start()

    def forward_block(way, step):
        zz = place(way, step)
        for group in range(2):
            core_copy(way, step, group, zz, 1 - c).wait_recv()

        @pl.when(zz < z)
        def _():
            forward_tile(zz * 4 * TOK, 0, False)
            forward_tile(zz * 4 * TOK + 2 * TOK, 2 * TOK, False)

        @pl.when(zz > z)
        def _():
            forward_tile(zz * 4 * TOK, 2 * TOK, False)

    arrive(0, 1, half > 1)
    arrive(1, 1, half > 2)
    for group in range(2):
        core_copy(0, 0, group, z, 1 - c).wait_recv()
    forward_tile(z * 4 * TOK, 0, True)
    forward_tile(z * 4 * TOK + 2 * TOK, 2 * TOK, True)

    def forward_step(step, carry):
        arrive(0, step, step < half)
        arrive(1, step, step < half - 1)
        forward_block(0, step - 1)
        forward_block(1, step - 1)
        return carry

    lax.fori_loop(2, half, forward_step, 0)
    arrive(0, half, False)
    forward_block(0, half - 1)
    forward_block(1, half - 1)
    forward_block(0, half)

    do_copy.wait_recv()
    turn(do_rows, do_cols)
    attended = (acc[...] / total[...]).astype(BF16)
    delta[...] = jnp.sum(
        do_cols[...].astype(F32) * attended.astype(F32), axis=0, keepdims=True
    )
    top[...] = top[...] + jnp.log2(total[...])
    for block in range(4):
        span = slice(block * TOK, (block + 1) * TOK)
        att_rows[span, :] = attended[:, span].T
    att_copy = copy_once(ATT_X, att_rows.at[peer_heads], att_own.at[own_heads], across)
    att_copy.start()
    att_own[own_heads, :] = att_rows[own_heads, :]

    def backward_tile(way, step, start, first_row, first_col, masked):
        span = slice(first_col, 4 * TOK)
        block = rows(start, 2 * TOK)
        keys = kv[block, :HD]
        probs = jnp.exp2(dot(keys, q_cols[:, span]) * scale_two - top[:, span])
        if masked:
            probs = jnp.where(own_mask(first_col), probs, 0.0)
        grad_prob = dot(kv[block, HD:], do_cols[:, span])
        grad_score = (probs * (grad_prob - delta[:, span]) * scale).astype(BF16)
        dq_cols[:, span] += dot_first(keys, grad_score)
        out = slice(first_row, first_row + 2 * TOK)
        part[way, step, out, :HD] = dot(grad_score, q_rows[span, :])
        part[way, step, out, HD:] = dot(probs.astype(BF16), do_rows[span, :])

    def swap_copy(way, step, xx):
        return copy(
            part.at[way, step, rows((xx * 2 + 1 - c) * TOK)],
            part_core.at[way, step, rows(xx * TOK)],
            swap_send.at[way, step, xx],
            swap_recv.at[way, step, xx],
            other_core,
        )

    def backward_block(way, step):
        zz = place(1 - way, step)

        @pl.when(zz < z)
        def _():
            backward_tile(way, step, zz * 4 * TOK, 0, 0, False)
            backward_tile(way, step, zz * 4 * TOK + 2 * TOK, 2 * TOK, 2 * TOK, False)

        @pl.when(zz > z)
        def _():
            backward_tile(way, step, zz * 4 * TOK, 0, 2 * TOK, False)
            part[way, step, 2 * TOK :, :] = jnp.zeros((2 * TOK, 2 * HD), F32)

        for xx in range(2):
            swap_copy(way, step, xx).start()

    def reduce_copy(way, step, xx):
        return copy(
            ring_out.at[way, step, rows(xx * TOK)],
            ring_in.at[way, step - 1, rows(xx * TOK)],
            reduce_send.at[way, step, xx],
            reduce_recv.at[way, step - 1, xx],
            along[way],
        )

    def pair_sum(way, step, xx):
        swap_copy(way, step, xx).wait_recv()
        return part[way, step, rows((xx * 2 + c) * TOK), :] + part_core[way, step, rows(xx * TOK), :]

    def reduce_step(way, step, farthest):
        for xx in range(2):
            summed = pair_sum(way, step, xx)

            @pl.when(step < farthest)
            def _():
                reduce_copy(way, step + 1, xx).wait_recv()

            summed = summed + ring_in[way, step, rows(xx * TOK), :].astype(F32)
            ring_out[way, step, rows(xx * TOK), :] = summed.astype(BF16)
            reduce_copy(way, step, xx).start()

    backward_block(0, half)
    backward_block(0, half - 1)
    backward_block(1, half - 1)
    reduce_step(0, half, half)

    def backward_step(count, carry):
        step = half - count
        backward_block(0, step)
        backward_block(1, step)
        reduce_step(0, step + 1, half)
        reduce_step(1, step + 1, half - 1)
        return carry

    lax.fori_loop(2, half, backward_step, 0)
    backward_tile(0, 0, z * 4 * TOK, 0, 0, True)
    backward_tile(0, 0, z * 4 * TOK + 2 * TOK, 2 * TOK, 2 * TOK, True)
    for xx in range(2):
        swap_copy(0, 0, xx).start()
    reduce_step(0, 1, half)
    reduce_step(1, 1, half - 1)

    for block in range(4):
        span = slice(block * TOK, (block + 1) * TOK)
        dq_rows[span, :] = dq_cols[:, span].T
    dq_copy = copy_once(DQ_X, dq_rows.at[peer_heads], dq_own.at[own_heads], across)
    dq_copy.start()
    dq_own[own_heads, :] = dq_rows[own_heads, :]

    att_copy.wait_recv()
    result = codes_in[...].astype(F32)
    for head in range(4):
        span = slice(head * TOK, (head + 1) * TOK)
        result = result + dot(att_own[span, :], w_out[span, :])
    out_codes[...] = result.astype(BF16)

    for xx in range(2):
        summed = pair_sum(0, 0, xx)
        for way in range(2):
            reduce_copy(way, 1, xx).wait_recv()
            summed = summed + ring_in[way, 0, rows(xx * TOK), :].astype(F32)
        kv_total[xx] = summed
    dkv_copy = copy_once(DKV_X, kv_total.at[1 - x], kv_peer, across)
    dkv_copy.start()

    dq_copy.wait_recv()
    normed_grad = jnp.zeros((TOK, w_query.shape[0]), F32)
    for head in range(4):
        span = slice(head * TOK, (head + 1) * TOK)
        lin_grad = norm_back(q_lin[:, span], q_gain[...], dq_own[span, :])
        normed_grad = normed_grad + dot_last(lin_grad, w_query[:, span])
    dkv_copy.wait_recv()
    kv_grad = kv_total[x] + kv_peer[...]
    key_grad = norm_back(k_lin[...], k_gain[...], kv_grad[:, :HD])
    normed_grad = normed_grad + dot_last(key_grad, w_key[...])
    normed_grad = normed_grad + dot_last(kv_grad[:, HD:].astype(BF16), w_value[...])
    wide = codes_in[...].astype(F32)
    inv_norm = lax.rsqrt(jnp.sum(wide * wide, axis=-1, keepdims=True) / D + NORM_EPS)
    inner = jnp.sum(wide * normed_grad, axis=-1, keepdims=True)
    in_grads[...] = (
        grads_in[...].astype(F32)
        + inv_norm * normed_grad
        - wide * (inv_norm * inv_norm * inv_norm) * inner / D
    ).astype(BF16)

    for once in (codes_copy, grads_copy, kv_copy, q_copy, do_copy, att_copy, dq_copy, dkv_copy):
        once.wait_send()

    def settle(way, step, gathers):
        for group in range(2):
            if gathers:
                gather_copy(way, step, group, z).wait_send()
                reduce_copy(way, step, group).wait_send()
            core_copy(way, step, group, z, c).wait_send()
            swap_copy(way, step, group).wait_send()

    settle(0, 0, False)

    def settle_both(step, carry):
        settle(0, step, True)
        settle(1, step, True)
        return carry

    lax.fori_loop(1, half, settle_both, 0)
    settle(0, half, True)


def rope_tables(positions, head_dim):
    half_dim = head_dim // 2
    exponent = jnp.arange(half_dim).astype(F32) * (2.0 / head_dim)
    frequency = jnp.power(F32(ROPE_BASE), -exponent)
    angles = positions.astype(F32)[:, None] * frequency[None, :]
    angles = jnp.concatenate([angles, angles], axis=-1)
    return (jnp.cos(angles), jnp.sin(angles))


def local(
    sent_codes, start_codes, sent_grads, loss_grads, w_query, w_key, w_value, w_out, q_gain, k_gain
):
    ring = lax.axis_size("seq") // 4
    sections = lax.axis_size("section")
    steps = ring // 2 + 1
    width = start_codes.shape[1]
    positions = lax.axis_index("seq") * TOK + jnp.arange(TOK, dtype=jnp.int32)
    cosines, sines = rope_tables(positions, HD)
    vmem = pltpu.VMEM
    dma = pltpu.SemaphoreType.DMA
    one_block = (TOK, width)
    heads = (4 * TOK, HD)
    columns = (HD, 4 * TOK)
    stat = (1, 4 * TOK)
    results = pl.pallas_call(
        functools.partial(kernel, ring, sections),
        out_shape=(jax.ShapeDtypeStruct(one_block, BF16),) * 2,
        in_specs=[pl.BlockSpec(memory_space=vmem)] * 12,
        out_specs=(pl.BlockSpec(memory_space=vmem),) * 2,
        scratch_shapes=[
            vmem(one_block, BF16),
            vmem(one_block, BF16),
            vmem(one_block, BF16),
            vmem(one_block, BF16),
            vmem(one_block, F32),
            vmem((TOK, HD), F32),
            vmem(heads, BF16),
            vmem(heads, BF16),
            vmem(columns, BF16),
            vmem(heads, BF16),
            vmem(heads, BF16),
            vmem(columns, BF16),
            vmem((ring * 4 * TOK, 2 * HD), BF16),
            vmem(stat, F32),
            vmem(stat, F32),
            vmem(columns, F32),
            vmem(stat, F32),
            vmem(heads, BF16),
            vmem(heads, BF16),
            vmem(columns, F32),
            vmem(heads, F32),
            vmem(heads, F32),
            vmem((2, steps, 4 * TOK, 2 * HD), F32),
            vmem((2, steps, 2 * TOK, 2 * HD), F32),
            vmem((2, steps, 2 * TOK, 2 * HD), BF16),
            vmem((2, steps, 2 * TOK, 2 * HD), BF16),
            vmem((2, TOK, 2 * HD), F32),
            vmem((TOK, 2 * HD), F32),
            dma((8,)),
            dma((8,)),
            dma((2, steps, 2)),
            dma((2, steps, 2)),
            dma((2, steps, 2)),
            dma((2, steps, 2)),
            dma((2, steps, 2)),
            dma((2, steps, 2)),
            dma((2, steps, 2)),
            dma((2, steps, 2)),
        ],
        compiler_params=pltpu.CompilerParams(
            collective_id=0, has_side_effects=True, vmem_limit_bytes=48 * 1024 * 1024
        ),
    )(
        sent_codes[0],
        start_codes,
        sent_grads[0],
        loss_grads,
        w_query[0],
        w_key[0],
        w_value[0],
        w_out[0],
        q_gain,
        k_gain,
        cosines,
        sines,
    )
    return (results[0][None], results[1][None])


def solution(mesh):
    in_specs = (
        P("section", "seq", None),
        P("seq", None),
        P("section", "seq", None),
        P("seq", None),
        P("section", None, None),
        P("section", None, None),
        P("section", None, None),
        P("section", None, None),
        P("section", None),
        P("section", None),
    )
    out_specs = (P("section", "seq", None), P("section", "seq", None))
    return jax.shard_map(local, mesh=mesh, in_specs=in_specs, out_specs=out_specs, check_vma=False)
```

time: 711 us -> 111 us (0.16)
  waiting for transfers between devices: 496 us -> 0 us
  Pallas kernels: 0 us -> 102 us
  starting transfers between devices: 70.7 us -> 0 us
  matrix products: 68.8 us -> 0 us
  local copies, waits for them, and re-layouts: 37.8 us -> 7.71 us
  other arithmetic: 18.9 us -> 0.4 us
  between operations: 14.3 us -> 0.71 us
    all_to_all x1 -> x0, waiting for transfers between devices: 364 us -> none  [local(): lax.all_to_all(key_part.reshape(seq_total, 1, 2 * head_dim), 'seq', split...]
    all_gather x1 -> x0, waiting for transfers between devices: 122 us -> none  [local(): lax.all_gather(key_rows, 'seq', axis=0, tiled=True)]
    pallas_call x0 -> x1, Pallas kernels: none -> 102 us  [local(): pl.pallas_call(functools.partial(kernel, ring, sections), out_shape=(jax....]
    dot_general x71 -> x0, matrix products: 68.8 us -> none  [the longest x18 22.9 us: scores_for(): lax.dot_general(query_flat, piece[:, :head_dim], contract_last, preferred...]
    all_to_all x1 -> x0, starting transfers between devices: 63.8 us -> none  [local(): lax.all_to_all(key_part.reshape(seq_total, 1, 2 * head_dim), 'seq', split...]
    reshape x4 -> x0, local copies, waits for them, and re-layouts: 18.4 us -> none  [the longest x1 18.1 us: local(): key_part.reshape(seq_total, 1, 2 * head_dim)]
    ppermute x2 -> x0, waiting for transfers between devices: 10.1 us -> none  [from_behind(): return lax.ppermute(block, axis, route)]
    dynamic_update_slice x9 -> x0, other arithmetic: 7.72 us -> none  [backward_work(): lax.dynamic_update_slice_in_dim(key_part, jnp.concatenate([key_grad, valu...]
  transfers between devices with their start and end apart: 4 -> 0, of which waited for: 4 -> 0; matrix products, arithmetic and copies ran while one was open for 1% -> 0% of each run, Pallas kernels for 0% -> 0%
where the time goes in v1:
time: 111 us; the launch traced here: 110 us
  Pallas kernels  102 us (92%)
  local copies, waits for them, and re-layouts  7.71 us (7%)
    pallas_call x1, Pallas kernels, local(): pl.pallas_call(functools.partial(kernel, ring, sections), out_shape=(jax....  102 us
    unnamed x22, local copies, waits for them, and re-layouts  7.71 us

profile of v1, /device:TPU:6, one launch (start us, length us, event | category | flops | bytes accessed | tf_op | source)
XLA Modules:
  0.0 110.4 jit_solution(4583646373764280919)
XLA Ops:
  0.7 0.0 copy-start.2
  0.7 0.0 copy-start.3
  0.7 0.1 broadcast_multiply_fusion
  0.8 0.3 fusion
  1.1 0.0 copy-start.8
  1.1 0.0 copy-start.9
  1.1 0.5 copy-done.2
  1.6 0.1 copy-done.3
  1.6 0.1 copy-done.8
  1.8 0.0 copy-done.9
  1.8 0.0 copy-start
  1.8 1.0 copy-done
  2.8 0.0 copy-start.1
  2.8 1.0 copy-done.1
  3.9 0.0 copy-start.4
  3.9 0.9 copy-done.4
  4.8 0.0 copy-start.5
  4.8 0.9 copy-done.5
  5.7 0.0 copy-start.6
  5.7 0.9 copy-done.6
  6.6 0.9 copy-done.7
  7.5 101.6 %shard_map.113 = (bf16[128,512]{1,0:T(8,128)(2,1)S(1)}, bf16[128,512]{1,0:T(8,128)(2,1)S(1)}) custom-call(bf16[128,512]{1,0:T(8,128)(2,1)S(1)} %bitcast.10, bf16[128,512]{1,0:T(8,128)(2,1)S(1)} %copy-done.3, bf16[128,512]{1,0:T(8,128)(2,1)S(1)} %bitcast.11, bf16[128,512]{1,0:T(8,128)(2,1)S(1)} %copy-done.5, bf16[512,512]{1,0:T(8,128)(2,1)S(1)} %bitcast.8, ...), custom_call_target="tpu_custom_call" | custom-call | tf_op jit(solution)/shard_map/pallas_call | solution.py:507
  109.1 0.7 copy.14
  109.8 0.7 copy.15
  (3 shorter events, 0.0 us)
Async XLA Ops:
  0.7 0.9 copy-start.2
  0.7 1.0 copy-start.3
  1.1 0.7 copy-start.8
  1.1 0.7 copy-start.9
  1.8 1.0 copy-start
  2.8 1.0 copy-start.1
  3.9 0.9 copy-start.4
  4.8 0.9 copy-start.5
  5.7 0.9 copy-start.6
  6.6 0.9 copy-start.7

commit v2 on v1

--- a/solution.py
+++ b/solution.py
@@ -46,16 +46,22 @@
     start_codes,
     sent_grads,
     loss_grads,
-    w_query,
-    w_key,
-    w_value,
-    w_out,
+    w_query_hbm,
+    w_key_hbm,
+    w_value_hbm,
+    w_out_hbm,
     q_gain,
     k_gain,
     cosines,
     sines,
     out_codes,
     in_grads,
+    w_query,
+    w_key,
+    w_value,
+    w_out,
+    codes_edge,
+    grads_edge,
     codes_buf,
     grads_buf,
     codes_in,
@@ -83,6 +89,7 @@
     ring_out,
     ring_in,
     kv_total,
+    kv_send,
     kv_peer,
     once_send,
     once_recv,
@@ -94,6 +101,7 @@
     reduce_recv,
     swap_send,
     swap_recv,
+    load_sems,
 ):
     half = ring // 2
     sec = lax.axis_index("section")
@@ -124,6 +132,22 @@
     def copy_once(number, src, dst, target):
         return copy(src, dst, once_send.at[number], once_recv.at[number], target)
 
+    loads = [
+        pltpu.make_async_copy(src, dst, load_sems.at[number])
+        for number, (src, dst) in enumerate(
+            (
+                (start_codes, codes_edge),
+                (w_key_hbm, w_key),
+                (w_value_hbm, w_value),
+                (w_query_hbm, w_query),
+                (loss_grads, grads_edge),
+                (w_out_hbm, w_out),
+            )
+        )
+    ]
+    for load in loads:
+        load.start()
+
     barrier = pltpu.get_barrier_semaphore()
     for partner in (along[0], along[1], other_core, across, next_section, last_section):
         pl.semaphore_signal(barrier, inc=1, device_id=partner, device_id_type=MESH)
@@ -132,7 +156,6 @@
     codes_copy = copy_once(CODES, sent_codes, codes_buf, next_section)
     grads_copy = copy_once(GRADS, sent_grads, grads_buf, last_section)
     codes_copy.start()
-    grads_copy.start()
 
     top[...] = jnp.full(top.shape, MASK_FILL, F32)
     total[...] = jnp.zeros(total.shape, F32)
@@ -179,11 +202,13 @@
         sems = (core_send.at[way, step, group], core_recv.at[way, step, group])
         return copy(ref, ref, *sems, other_core)
 
+    for load in loads[:3]:
+        load.wait()
     codes_copy.wait_recv()
 
     @pl.when(sec == 0)
     def _():
-        codes_in[...] = start_codes[...]
+        codes_in[...] = codes_edge[...]
 
     @pl.when(sec != 0)
     def _():
@@ -204,6 +229,7 @@
         gather_copy(way, 1, 0, z).start()
     core_copy(0, 0, 0, z, c).start()
 
+    loads[3].wait()
     q_lin[...] = dot(normed, w_query[...])
     for head in range(4):
         q_own[head * TOK : (head + 1) * TOK, :] = head_norm(
@@ -219,23 +245,7 @@
     for way in range(2):
         gather_copy(way, 1, 1, z).start()
     core_copy(0, 0, 1, z, c).start()
-
-    grads_copy.wait_recv()
-
-    @pl.when(sec == sections - 1)
-    def _():
-        grads_in[...] = loss_grads[...]
-
-    @pl.when(sec != sections - 1)
-    def _():
-        grads_in[...] = grads_buf[...]
-
-    grad_att = dot_last(grads_in[...], w_out[...]).astype(BF16)
-    for head in range(4):
-        do_own[head * TOK : (head + 1) * TOK, :] = grad_att[:, head * HD : (head + 1) * HD]
-    do_copy = copy_once(DO_X, do_own.at[peer_heads], do_rows.at[own_heads], across)
-    do_copy.start()
-    do_rows[own_heads, :] = do_own[own_heads, :]
+    grads_copy.start()
 
     def turn(src, dst):
         for block in range(4):
@@ -296,17 +306,36 @@
         def _():
             forward_tile(zz * 4 * TOK, 2 * TOK, False)
 
-    arrive(0, 1, half > 1)
-    arrive(1, 1, half > 2)
     for group in range(2):
         core_copy(0, 0, group, z, 1 - c).wait_recv()
     forward_tile(z * 4 * TOK, 0, True)
+    arrive(0, 1, half > 1)
+    arrive(1, 1, half > 2)
     forward_tile(z * 4 * TOK + 2 * TOK, 2 * TOK, True)
+
+    for load in loads[4:]:
+        load.wait()
+    grads_copy.wait_recv()
+
+    @pl.when(sec == sections - 1)
+    def _():
+        grads_in[...] = grads_edge[...]
+
+    @pl.when(sec != sections - 1)
+    def _():
+        grads_in[...] = grads_buf[...]
+
+    grad_att = dot_last(grads_in[...], w_out[...]).astype(BF16)
+    for head in range(4):
+        do_own[head * TOK : (head + 1) * TOK, :] = grad_att[:, head * HD : (head + 1) * HD]
+    do_copy = copy_once(DO_X, do_own.at[peer_heads], do_rows.at[own_heads], across)
+    do_copy.start()
+    do_rows[own_heads, :] = do_own[own_heads, :]
 
     def forward_step(step, carry):
         arrive(0, step, step < half)
+        forward_block(0, step - 1)
         arrive(1, step, step < half - 1)
-        forward_block(0, step - 1)
         forward_block(1, step - 1)
         return carry
 
@@ -395,16 +424,16 @@
             reduce_copy(way, step, xx).start()
 
     backward_block(0, half)
-    backward_block(0, half - 1)
     backward_block(1, half - 1)
     reduce_step(0, half, half)
+    backward_block(0, half - 1)
 
     def backward_step(count, carry):
         step = half - count
-        backward_block(0, step)
+        reduce_step(1, step + 1, half - 1)
         backward_block(1, step)
         reduce_step(0, step + 1, half)
-        reduce_step(1, step + 1, half - 1)
+        backward_block(0, step)
         return carry
 
     lax.fori_loop(2, half, backward_step, 0)
@@ -435,7 +464,8 @@
             reduce_copy(way, 1, xx).wait_recv()
             summed = summed + ring_in[way, 0, rows(xx * TOK), :].astype(F32)
         kv_total[xx] = summed
-    dkv_copy = copy_once(DKV_X, kv_total.at[1 - x], kv_peer, across)
+        kv_send[xx] = summed.astype(BF16)
+    dkv_copy = copy_once(DKV_X, kv_send.at[1 - x], kv_peer, across)
     dkv_copy.start()
 
     dq_copy.wait_recv()
@@ -445,7 +475,7 @@
         lin_grad = norm_back(q_lin[:, span], q_gain[...], dq_own[span, :])
         normed_grad = normed_grad + dot_last(lin_grad, w_query[:, span])
     dkv_copy.wait_recv()
-    kv_grad = kv_total[x] + kv_peer[...]
+    kv_grad = kv_total[x] + kv_peer[...].astype(F32)
     key_grad = norm_back(k_lin[...], k_gain[...], kv_grad[:, :HD])
     normed_grad = normed_grad + dot_last(key_grad, w_key[...])
     normed_grad = normed_grad + dot_last(kv_grad[:, HD:].astype(BF16), w_value[...])
@@ -507,9 +537,15 @@
     results = pl.pallas_call(
         functools.partial(kernel, ring, sections),
         out_shape=(jax.ShapeDtypeStruct(one_block, BF16),) * 2,
-        in_specs=[pl.BlockSpec(memory_space=vmem)] * 12,
+        in_specs=[pl.BlockSpec(memory_space=pltpu.HBM)] * 8 + [pl.BlockSpec(memory_space=vmem)] * 4,
         out_specs=(pl.BlockSpec(memory_space=vmem),) * 2,
         scratch_shapes=[
+            vmem(w_query.shape[1:], BF16),
+            vmem(w_key.shape[1:], BF16),
+            vmem(w_value.shape[1:], BF16),
+            vmem(w_out.shape[1:], BF16),
+            vmem(one_block, BF16),
+            vmem(one_block, BF16),
             vmem(one_block, BF16),
             vmem(one_block, BF16),
             vmem(one_block, BF16),
@@ -537,7 +573,8 @@
             vmem((2, steps, 2 * TOK, 2 * HD), BF16),
             vmem((2, steps, 2 * TOK, 2 * HD), BF16),
             vmem((2, TOK, 2 * HD), F32),
-            vmem((TOK, 2 * HD), F32),
+            vmem((2, TOK, 2 * HD), BF16),
+            vmem((TOK, 2 * HD), BF16),
             dma((8,)),
             dma((8,)),
             dma((2, steps, 2)),
@@ -548,9 +585,10 @@
             dma((2, steps, 2)),
             dma((2, steps, 2)),
             dma((2, steps, 2)),
+            dma((6,)),
         ],
         compiler_params=pltpu.CompilerParams(
-            collective_id=0, has_side_effects=True, vmem_limit_bytes=48 * 1024 * 1024
+            collective_id=0, has_side_effects=True, vmem_limit_bytes=60 * 1024 * 1024
         ),
     )(
         sent_codes[0],

time: 111 us -> 102 us (0.919)
  local copies, waits for them, and re-layouts: 7.71 us -> 2.26 us
  Pallas kernels: 102 us -> 97.2 us
    unnamed x22 -> x4, local copies, waits for them, and re-layouts: 7.71 us -> 2.26 us
    pallas_call x1, Pallas kernels: 102 us -> 97.2 us  [local(): pl.pallas_call(functools.partial(kernel, ring, sections), out_shape=(jax....]
where the time goes in v2:
time: 102 us; the launch traced here: 101 us
  Pallas kernels  97.2 us (95%)
  local copies, waits for them, and re-layouts  2.26 us (2%)
  other arithmetic  1.06 us (1%)
    pallas_call x1, Pallas kernels, local(): pl.pallas_call(functools.partial(kernel, ring, sections), out_shape=(jax....  97.2 us
    unnamed x4, local copies, waits for them, and re-layouts  2.26 us

profile of v2, /device:TPU:6, one launch (start us, length us, event | category | flops | bytes accessed | tf_op | source)
XLA Modules:
  0.0 101.2 jit_solution(3637422217412868304)
XLA Ops:
  0.7 0.1 broadcast_multiply_fusion
  0.7 1.0 fusion
  1.7 97.2 %shard_map.113 = (bf16[128,512]{1,0:T(8,128)(2,1)}, bf16[128,512]{1,0:T(8,128)(2,1)}) custom-call(bf16[128,512]{1,0:T(8,128)(2,1)} %bitcast.10, bf16[128,512]{1,0:T(8,128)(2,1)} %start_codes.1, bf16[128,512]{1,0:T(8,128)(2,1)} %bitcast.11, bf16[128,512]{1,0:T(8,128)(2,1)} %loss_grads.1, bf16[512,512]{1,0:T(8,128)(2,1)} %bitcast.8, ...), custom_call_target="tpu_custom_call" | custom-call | tf_op jit(solution)/shard_map/pallas_call | solution.py:537
  99.0 0.0 copy-start
  99.0 1.6 %copy.14 = bf16[1,128,512]{2,1,0:T(8,128)(2,1)} copy(bf16[1,128,512]{2,1,0:T(8,128)(2,1)} %bitcast.15) | data formatting | bytes 262144
  100.6 0.0 copy-done
  100.6 0.7 copy.15
  (2 shorter events, 0.0 us)
Async XLA Ops:
  99.0 1.6 %copy-start = (bf16[128,512]{1,0:T(8,128)(2,1)S(1)}, bf16[128,512]{1,0:T(8,128)(2,1)}, u32[]{:S(2)}) copy-start(bf16[128,512]{1,0:T(8,128)(2,1)} %get-tuple-element.5) | copy-start | bytes 393220

commit v3 on v2

--- a/solution.py
+++ b/solution.py
@@ -17,6 +17,7 @@
 BF16 = jnp.bfloat16
 TOK = 128
 HD = 128
+CUT = 48
 CONTRACT_LAST = (((1,), (1,)), ((), ()))
 CONTRACT_FIRST = (((0,), (0,)), ((), ()))
 
@@ -84,11 +85,14 @@
     dq_cols,
     dq_rows,
     dq_own,
+    kept_scores,
     part,
     part_core,
     ring_out,
     ring_in,
-    kv_total,
+    cross_out,
+    cross_in,
+    kv_grad,
     kv_send,
     kv_peer,
     once_send,
@@ -101,6 +105,10 @@
     reduce_recv,
     swap_send,
     swap_recv,
+    relay_send,
+    relay_recv,
+    cross_send,
+    cross_recv,
     load_sems,
 ):
     half = ring // 2
@@ -183,24 +191,29 @@
         inner = jnp.mean(tensor * scaled, axis=-1, keepdims=True)
         return (inv * scaled - tensor * (inv * inv * inv) * inner).astype(BF16)
 
-    def chunk(zz, xx, cc):
-        return kv.at[rows(((zz * 2 + xx) * 2 + cc) * TOK)]
+    def piece_of(piece, zz, cc, xx=None):
+        if xx is None:
+            xx = x if piece == 0 else 1 - x
+        first, count = ((0, TOK), (0, CUT), (CUT, TOK - CUT))[piece]
+        start = ((zz * 2 + xx) * 2 + cc) * TOK + first
+        return kv.at[pl.ds(pl.multiple_of(start, 16), count)]
 
     def place(way, step):
         return lax.rem(z + (ring - step if way == 0 else step), ring)
 
-    def group_x(group):
-        return x if group == 0 else 1 - x
-
-    def gather_copy(way, step, group, zz):
-        ref = chunk(zz, group_x(group), c)
-        sems = (gather_send.at[way, step, group], gather_recv.at[way, step, group])
+    def gather_copy(way, step, piece, zz):
+        ref = piece_of(piece, zz, c)
+        sems = (gather_send.at[way, step, piece], gather_recv.at[way, step, piece])
         return copy(ref, ref, *sems, along[way])
 
-    def core_copy(way, step, group, zz, cc):
-        ref = chunk(zz, group_x(group), cc)
-        sems = (core_send.at[way, step, group], core_recv.at[way, step, group])
+    def core_copy(way, step, piece, zz, cc):
+        ref = piece_of(piece, zz, cc)
+        sems = (core_send.at[way, step, piece], core_recv.at[way, step, piece])
         return copy(ref, ref, *sems, other_core)
+
+    def relay_copy(way, step, zz, xx):
+        ref = piece_of(2, zz, c, xx)
+        return copy(ref, ref, relay_send.at[way, step], relay_recv.at[way, step], across)
 
     for load in loads[:3]:
         load.wait()
@@ -223,8 +236,10 @@
     kv[own, :HD] = head_norm(key_lin, k_gain[...])
     kv[own, HD:] = dot(normed, w_value[...]).astype(BF16)
 
-    kv_copy = copy_once(KV_X, chunk(z, x, c), chunk(z, x, c), across)
+    first_piece = piece_of(1, z, c, x)
+    kv_copy = copy_once(KV_X, first_piece, first_piece, across)
     kv_copy.start()
+    relay_copy(0, 0, z, x).start()
     for way in range(2):
         gather_copy(way, 1, 0, z).start()
     core_copy(0, 0, 0, z, c).start()
@@ -245,6 +260,8 @@
     for way in range(2):
         gather_copy(way, 1, 1, z).start()
     core_copy(0, 0, 1, z, c).start()
+    relay_copy(0, 0, z, 1 - x).wait_recv()
+    core_copy(0, 0, 2, z, c).start()
     grads_copy.start()
 
     def turn(src, dst):
@@ -267,12 +284,13 @@
             visible = visible | (col >= 2 * TOK)
         return visible
 
-    def forward_tile(start, first_col, masked):
+    def forward_tile(way, step, zz, xx, first_col, masked):
         span = slice(first_col, 4 * TOK)
-        block = rows(start, 2 * TOK)
+        block = rows((zz * 2 + xx) * 2 * TOK, 2 * TOK)
         scores = dot(kv[block, :HD], q_cols[:, span]) * scale_two
         if masked:
             scores = jnp.where(own_mask(first_col), scores, 2 * MASK_FILL)
+        kept_scores[way, step, xx * 2 * TOK : (xx + 1) * 2 * TOK, span] = scores
         top_old = top[:, span]
         top_new = jnp.maximum(top_old, jnp.max(scores, axis=0, keepdims=True))
         weights = jnp.exp2(scores - top_new)
@@ -283,35 +301,42 @@
 
     def arrive(way, step, forward):
         zz = place(way, step)
-        for group in range(2):
-            gather_copy(way, step, group, zz).wait_recv()
+        for piece in range(2):
+            gather_copy(way, step, piece, zz).wait_recv()
 
             @pl.when(forward)
             def _():
-                gather_copy(way, step + 1, group, zz).start()
-
-            core_copy(way, step, group, zz, c).start()
+                gather_copy(way, step + 1, piece, zz).start()
+
+            if piece == 0:
+                relay_copy(way, step, zz, x).start()
+            core_copy(way, step, piece, zz, c).start()
+
+    def arrive_across(way, step):
+        zz = place(way, step)
+        relay_copy(way, step, zz, 1 - x).wait_recv()
+        core_copy(way, step, 2, zz, c).start()
 
     def forward_block(way, step):
         zz = place(way, step)
-        for group in range(2):
-            core_copy(way, step, group, zz, 1 - c).wait_recv()
+        for piece in range(3):
+            core_copy(way, step, piece, zz, 1 - c).wait_recv()
 
         @pl.when(zz < z)
         def _():
-            forward_tile(zz * 4 * TOK, 0, False)
-            forward_tile(zz * 4 * TOK + 2 * TOK, 2 * TOK, False)
+            forward_tile(way, step, zz, 0, 0, False)
+            forward_tile(way, step, zz, 1, 2 * TOK, False)
 
         @pl.when(zz > z)
         def _():
-            forward_tile(zz * 4 * TOK, 2 * TOK, False)
-
-    for group in range(2):
-        core_copy(0, 0, group, z, 1 - c).wait_recv()
-    forward_tile(z * 4 * TOK, 0, True)
+            forward_tile(way, step, zz, 0, 2 * TOK, False)
+
+    for piece in range(3):
+        core_copy(0, 0, piece, z, 1 - c).wait_recv()
+    forward_tile(0, 0, z, 0, 0, True)
     arrive(0, 1, half > 1)
     arrive(1, 1, half > 2)
-    forward_tile(z * 4 * TOK + 2 * TOK, 2 * TOK, True)
+    forward_tile(0, 0, z, 1, 2 * TOK, True)
 
     for load in loads[4:]:
         load.wait()
@@ -334,14 +359,25 @@
 
     def forward_step(step, carry):
         arrive(0, step, step < half)
+        arrive_across(0, step - 1)
+
+        @pl.when(step > 2)
+        def _():
+            forward_block(1, step - 2)
+
+        arrive(1, step, step < half - 1)
+        arrive_across(1, step - 1)
         forward_block(0, step - 1)
-        arrive(1, step, step < half - 1)
-        forward_block(1, step - 1)
         return carry
 
     lax.fori_loop(2, half, forward_step, 0)
     arrive(0, half, False)
+    arrive_across(0, half - 1)
+    if half > 2:
+        forward_block(1, half - 2)
+    arrive_across(1, half - 1)
     forward_block(0, half - 1)
+    arrive_across(0, half)
     forward_block(1, half - 1)
     forward_block(0, half)
 
@@ -359,19 +395,16 @@
     att_copy.start()
     att_own[own_heads, :] = att_rows[own_heads, :]
 
-    def backward_tile(way, step, start, first_row, first_col, masked):
+    def backward_tile(way, step, came, zz, xx, first_col):
         span = slice(first_col, 4 * TOK)
-        block = rows(start, 2 * TOK)
-        keys = kv[block, :HD]
-        probs = jnp.exp2(dot(keys, q_cols[:, span]) * scale_two - top[:, span])
-        if masked:
-            probs = jnp.where(own_mask(first_col), probs, 0.0)
+        block = rows((zz * 2 + xx) * 2 * TOK, 2 * TOK)
+        out = slice(xx * 2 * TOK, (xx + 1) * 2 * TOK)
+        probs = jnp.exp2(kept_scores[came, step, out, span] - top[:, span])
         grad_prob = dot(kv[block, HD:], do_cols[:, span])
         grad_score = (probs * (grad_prob - delta[:, span]) * scale).astype(BF16)
-        dq_cols[:, span] += dot_first(keys, grad_score)
-        out = slice(first_row, first_row + 2 * TOK)
+        part[way, step, out, HD:] = dot(probs.astype(BF16), do_rows[span, :])
         part[way, step, out, :HD] = dot(grad_score, q_rows[span, :])
-        part[way, step, out, HD:] = dot(probs.astype(BF16), do_rows[span, :])
+        dq_cols[:, span] += dot_first(kv[block, :HD], grad_score)
 
     def swap_copy(way, step, xx):
         return copy(
@@ -382,67 +415,103 @@
             other_core,
         )
 
-    def backward_block(way, step):
+    def backward_block(way, step, came=None):
         zz = place(1 - way, step)
+        came = 1 - way if came is None else came
 
         @pl.when(zz < z)
         def _():
-            backward_tile(way, step, zz * 4 * TOK, 0, 0, False)
-            backward_tile(way, step, zz * 4 * TOK + 2 * TOK, 2 * TOK, 2 * TOK, False)
+            backward_tile(way, step, came, zz, 0, 0)
+            backward_tile(way, step, came, zz, 1, 2 * TOK)
 
         @pl.when(zz > z)
         def _():
-            backward_tile(way, step, zz * 4 * TOK, 0, 2 * TOK, False)
+            backward_tile(way, step, came, zz, 0, 2 * TOK)
             part[way, step, 2 * TOK :, :] = jnp.zeros((2 * TOK, 2 * HD), F32)
 
         for xx in range(2):
             swap_copy(way, step, xx).start()
 
-    def reduce_copy(way, step, xx):
+    def pair_sum(way, step, xx, first, count):
+        mine = pl.ds(pl.multiple_of((xx * 2 + c) * TOK + first, 16), count)
+        theirs = pl.ds(pl.multiple_of(xx * TOK + first, 16), count)
+        return part[way, step, mine, :] + part_core[way, step, theirs, :]
+
+    def cross_copy(way, step):
         return copy(
-            ring_out.at[way, step, rows(xx * TOK)],
-            ring_in.at[way, step - 1, rows(xx * TOK)],
-            reduce_send.at[way, step, xx],
-            reduce_recv.at[way, step - 1, xx],
+            cross_out.at[way, step],
+            cross_in.at[way, step],
+            cross_send.at[way, step],
+            cross_recv.at[way, step],
+            across,
+        )
+
+    def cross_step(way, step):
+        for xx in range(2):
+            swap_copy(way, step, xx).wait_recv()
+        cross_out[way, step] = pair_sum(way, step, 1 - x, CUT, TOK - CUT).astype(BF16)
+        cross_copy(way, step).start()
+
+    group_rows = (slice(0, TOK), slice(TOK, TOK + CUT))
+
+    def reduce_copy(way, step, group):
+        return copy(
+            ring_out.at[way, step, group_rows[group]],
+            ring_in.at[way, step - 1, group_rows[group]],
+            reduce_send.at[way, step, group],
+            reduce_recv.at[way, step - 1, group],
             along[way],
         )
 
-    def pair_sum(way, step, xx):
-        swap_copy(way, step, xx).wait_recv()
-        return part[way, step, rows((xx * 2 + c) * TOK), :] + part_core[way, step, rows(xx * TOK), :]
-
     def reduce_step(way, step, farthest):
-        for xx in range(2):
-            summed = pair_sum(way, step, xx)
-
+        def arrived(group):
             @pl.when(step < farthest)
             def _():
-                reduce_copy(way, step + 1, xx).wait_recv()
-
-            summed = summed + ring_in[way, step, rows(xx * TOK), :].astype(F32)
-            ring_out[way, step, rows(xx * TOK), :] = summed.astype(BF16)
-            reduce_copy(way, step, xx).start()
-
-    backward_block(0, half)
+                reduce_copy(way, step + 1, group).wait_recv()
+
+        arrived(0)
+        ring_out[way, step, :CUT] = (
+            pair_sum(way, step, x, 0, CUT) + ring_in[way, step, :CUT].astype(F32)
+        ).astype(BF16)
+        cross_copy(way, step).wait_recv()
+        ring_out[way, step, CUT:TOK] = (
+            pair_sum(way, step, x, CUT, TOK - CUT)
+            + cross_in[way, step].astype(F32)
+            + ring_in[way, step, CUT:TOK].astype(F32)
+        ).astype(BF16)
+        reduce_copy(way, step, 0).start()
+        arrived(1)
+        ring_out[way, step, TOK:] = (
+            pair_sum(way, step, 1 - x, 0, CUT) + ring_in[way, step, TOK:].astype(F32)
+        ).astype(BF16)
+        reduce_copy(way, step, 1).start()
+
+    backward_block(0, half, 0)
     backward_block(1, half - 1)
+    cross_step(0, half)
+    backward_block(0, half - 1)
+    cross_step(1, half - 1)
     reduce_step(0, half, half)
-    backward_block(0, half - 1)
 
     def backward_step(count, carry):
         step = half - count
+        backward_block(1, step)
+        cross_step(0, step + 1)
         reduce_step(1, step + 1, half - 1)
-        backward_block(1, step)
+        backward_block(0, step)
+        cross_step(1, step)
         reduce_step(0, step + 1, half)
-        backward_block(0, step)
         return carry
 
     lax.fori_loop(2, half, backward_step, 0)
-    backward_tile(0, 0, z * 4 * TOK, 0, 0, True)
-    backward_tile(0, 0, z * 4 * TOK + 2 * TOK, 2 * TOK, 2 * TOK, True)
+    backward_tile(0, 0, 0, z, 0, 0)
+    backward_tile(0, 0, 0, z, 1, 2 * TOK)
     for xx in range(2):
         swap_copy(0, 0, xx).start()
+    cross_step(0, 1)
+    reduce_step(1, 1, half - 1)
+    cross_step(0, 0)
     reduce_step(0, 1, half)
-    reduce_step(1, 1, half - 1)
 
     for block in range(4):
         span = slice(block * TOK, (block + 1) * TOK)
@@ -458,14 +527,13 @@
         result = result + dot(att_own[span, :], w_out[span, :])
     out_codes[...] = result.astype(BF16)
 
-    for xx in range(2):
-        summed = pair_sum(0, 0, xx)
-        for way in range(2):
-            reduce_copy(way, 1, xx).wait_recv()
-            summed = summed + ring_in[way, 0, rows(xx * TOK), :].astype(F32)
-        kv_total[xx] = summed
-        kv_send[xx] = summed.astype(BF16)
-    dkv_copy = copy_once(DKV_X, kv_send.at[1 - x], kv_peer, across)
+    def ring_total(span):
+        return ring_in[0, 0, span].astype(F32) + ring_in[1, 0, span].astype(F32)
+
+    for way in range(2):
+        reduce_copy(way, 1, 1).wait_recv()
+    kv_send[...] = (pair_sum(0, 0, 1 - x, 0, CUT) + ring_total(group_rows[1])).astype(BF16)
+    dkv_copy = copy_once(DKV_X, kv_send, kv_peer, across)
     dkv_copy.start()
 
     dq_copy.wait_recv()
@@ -474,8 +542,16 @@
         span = slice(head * TOK, (head + 1) * TOK)
         lin_grad = norm_back(q_lin[:, span], q_gain[...], dq_own[span, :])
         normed_grad = normed_grad + dot_last(lin_grad, w_query[:, span])
+    for way in range(2):
+        reduce_copy(way, 1, 0).wait_recv()
+    cross_copy(0, 0).wait_recv()
+    kv_grad[CUT:, :] = (
+        pair_sum(0, 0, x, CUT, TOK - CUT) + ring_total(slice(CUT, TOK)) + cross_in[0, 0].astype(F32)
+    )
     dkv_copy.wait_recv()
-    kv_grad = kv_total[x] + kv_peer[...].astype(F32)
+    kv_grad[:CUT, :] = (
+        pair_sum(0, 0, x, 0, CUT) + ring_total(slice(0, CUT)) + kv_peer[...].astype(F32)
+    )
     key_grad = norm_back(k_lin[...], k_gain[...], kv_grad[:, :HD])
     normed_grad = normed_grad + dot_last(key_grad, w_key[...])
     normed_grad = normed_grad + dot_last(kv_grad[:, HD:].astype(BF16), w_value[...])
@@ -496,8 +572,11 @@
             if gathers:
                 gather_copy(way, step, group, z).wait_send()
                 reduce_copy(way, step, group).wait_send()
-            core_copy(way, step, group, z, c).wait_send()
             swap_copy(way, step, group).wait_send()
+        for piece in range(3):
+            core_copy(way, step, piece, z, c).wait_send()
+        relay_copy(way, step, z, x).wait_send()
+        cross_copy(way, step).wait_send()
 
     settle(0, 0, False)
 
@@ -568,23 +647,30 @@
             vmem(columns, F32),
             vmem(heads, F32),
             vmem(heads, F32),
+            vmem((2, steps, 4 * TOK, 4 * TOK), F32),
             vmem((2, steps, 4 * TOK, 2 * HD), F32),
             vmem((2, steps, 2 * TOK, 2 * HD), F32),
-            vmem((2, steps, 2 * TOK, 2 * HD), BF16),
-            vmem((2, steps, 2 * TOK, 2 * HD), BF16),
-            vmem((2, TOK, 2 * HD), F32),
-            vmem((2, TOK, 2 * HD), BF16),
-            vmem((TOK, 2 * HD), BF16),
+            vmem((2, steps, TOK + CUT, 2 * HD), BF16),
+            vmem((2, steps, TOK + CUT, 2 * HD), BF16),
+            vmem((2, steps, TOK - CUT, 2 * HD), BF16),
+            vmem((2, steps, TOK - CUT, 2 * HD), BF16),
+            vmem((TOK, 2 * HD), F32),
+            vmem((CUT, 2 * HD), BF16),
+            vmem((CUT, 2 * HD), BF16),
             dma((8,)),
             dma((8,)),
             dma((2, steps, 2)),
             dma((2, steps, 2)),
+            dma((2, steps, 3)),
+            dma((2, steps, 3)),
             dma((2, steps, 2)),
             dma((2, steps, 2)),
             dma((2, steps, 2)),
             dma((2, steps, 2)),
-            dma((2, steps, 2)),
-            dma((2, steps, 2)),
+            dma((2, steps)),
+            dma((2, steps)),
+            dma((2, steps)),
+            dma((2, steps)),
             dma((6,)),
         ],
         compiler_params=pltpu.CompilerParams(

time: 102 us -> 102 us (level); the launches traced: 101 us -> 100 us
    pallas_call x1, Pallas kernels: 97.2 us -> 96.2 us  [local(): pl.pallas_call(functools.partial(kernel, ring, sections), out_shape=(jax....]
where the time goes in v3:
time: 102 us; the launch traced here: 100 us
  Pallas kernels  96.2 us (94%)
  local copies, waits for them, and re-layouts  2.26 us (2%)
  other arithmetic  1.06 us (1%)
    pallas_call x1, Pallas kernels, local(): pl.pallas_call(functools.partial(kernel, ring, sections), out_shape=(jax....  96.2 us
    unnamed x4, local copies, waits for them, and re-layouts  2.26 us

profile of v3, /device:TPU:6, one launch (start us, length us, event | category | flops | bytes accessed | tf_op | source)
XLA Modules:
  0.0 100.2 jit_solution(406786189994479021)
XLA Ops:
  0.7 0.1 broadcast_multiply_fusion
  0.7 1.0 fusion
  1.7 96.2 %shard_map.113 = (bf16[128,512]{1,0:T(8,128)(2,1)}, bf16[128,512]{1,0:T(8,128)(2,1)}) custom-call(bf16[128,512]{1,0:T(8,128)(2,1)} %bitcast.10, bf16[128,512]{1,0:T(8,128)(2,1)} %start_codes.1, bf16[128,512]{1,0:T(8,128)(2,1)} %bitcast.11, bf16[128,512]{1,0:T(8,128)(2,1)} %loss_grads.1, bf16[512,512]{1,0:T(8,128)(2,1)} %bitcast.8, ...), custom_call_target="tpu_custom_call" | custom-call | tf_op jit(solution)/shard_map/pallas_call | solution.py:616
  97.9 0.0 copy-start
  97.9 1.6 %copy.14 = bf16[1,128,512]{2,1,0:T(8,128)(2,1)} copy(bf16[1,128,512]{2,1,0:T(8,128)(2,1)} %bitcast.15) | data formatting | bytes 262144
  99.5 0.0 copy-done
  99.5 0.7 copy.15
  (2 shorter events, 0.0 us)
Async XLA Ops:
  97.9 1.6 %copy-start = (bf16[128,512]{1,0:T(8,128)(2,1)S(1)}, bf16[128,512]{1,0:T(8,128)(2,1)}, u32[]{:S(2)}) copy-start(bf16[128,512]{1,0:T(8,128)(2,1)} %get-tuple-element.5) | copy-start | bytes 393220

commit v4 on v3

--- a/solution.py
+++ b/solution.py
@@ -121,7 +121,9 @@
     def device(xx, zz, cc):
         return (sec, (xx * ring + zz) * 2 + cc)
 
-    along = (device(x, lax.rem(z + 1, ring), c), device(x, lax.rem(z + ring - 1, ring), c))
+    def along(way):
+        return device(x, lax.rem(z + 1 + way * (ring - 2), ring), c)
+
     other_core = device(x, z, 1 - c)
     across = device(1 - x, z, c)
     next_section = (lax.rem(sec + 1, sections), me)
@@ -157,7 +159,7 @@
         load.start()
 
     barrier = pltpu.get_barrier_semaphore()
-    for partner in (along[0], along[1], other_core, across, next_section, last_section):
+    for partner in (along(0), along(1), other_core, across, next_section, last_section):
         pl.semaphore_signal(barrier, inc=1, device_id=partner, device_id_type=MESH)
     pl.semaphore_wait(barrier, 6)
 
@@ -199,12 +201,12 @@
         return kv.at[pl.ds(pl.multiple_of(start, 16), count)]
 
     def place(way, step):
-        return lax.rem(z + (ring - step if way == 0 else step), ring)
+        return lax.rem(z + way * step + (1 - way) * (ring - step), ring)
 
     def gather_copy(way, step, piece, zz):
         ref = piece_of(piece, zz, c)
         sems = (gather_send.at[way, step, piece], gather_recv.at[way, step, piece])
-        return copy(ref, ref, *sems, along[way])
+        return copy(ref, ref, *sems, along(way))
 
     def core_copy(way, step, piece, zz, cc):
         ref = piece_of(piece, zz, cc)
@@ -284,13 +286,13 @@
             visible = visible | (col >= 2 * TOK)
         return visible
 
-    def forward_tile(way, step, zz, xx, first_col, masked):
+    def forward_tile(kept, step, zz, xx, first_col, masked):
         span = slice(first_col, 4 * TOK)
         block = rows((zz * 2 + xx) * 2 * TOK, 2 * TOK)
         scores = dot(kv[block, :HD], q_cols[:, span]) * scale_two
         if masked:
             scores = jnp.where(own_mask(first_col), scores, 2 * MASK_FILL)
-        kept_scores[way, step, xx * 2 * TOK : (xx + 1) * 2 * TOK, span] = scores
+        kept_scores[kept, step, rows(xx * 2 * TOK, 2 * TOK), span] = scores
         top_old = top[:, span]
         top_new = jnp.maximum(top_old, jnp.max(scores, axis=0, keepdims=True))
         weights = jnp.exp2(scores - top_new)
@@ -317,24 +319,26 @@
         relay_copy(way, step, zz, 1 - x).wait_recv()
         core_copy(way, step, 2, zz, c).start()
 
-    def forward_block(way, step):
+    def gathered(item):
+        return lax.rem(item + 1, 2), lax.div(item + 1, 2)
+
+    def forward_block(item):
+        way, step = gathered(item)
         zz = place(way, step)
         for piece in range(3):
             core_copy(way, step, piece, zz, 1 - c).wait_recv()
+        kept = way + lax.div(step, half)
 
         @pl.when(zz < z)
         def _():
-            forward_tile(way, step, zz, 0, 0, False)
-            forward_tile(way, step, zz, 1, 2 * TOK, False)
-
-        @pl.when(zz > z)
-        def _():
-            forward_tile(way, step, zz, 0, 2 * TOK, False)
-
+            forward_tile(kept, step, zz, 0, 0, False)
+
+        forward_tile(kept, step, zz, jnp.where(zz < z, 1, 0), 2 * TOK, False)
+
+    arrive(0, 1, half > 1)
     for piece in range(3):
         core_copy(0, 0, piece, z, 1 - c).wait_recv()
     forward_tile(0, 0, z, 0, 0, True)
-    arrive(0, 1, half > 1)
     arrive(1, 1, half > 2)
     forward_tile(0, 0, z, 1, 2 * TOK, True)
 
@@ -357,29 +361,23 @@
     do_copy.start()
     do_rows[own_heads, :] = do_own[own_heads, :]
 
-    def forward_step(step, carry):
-        arrive(0, step, step < half)
-        arrive_across(0, step - 1)
-
-        @pl.when(step > 2)
-        def _():
-            forward_block(1, step - 2)
-
-        arrive(1, step, step < half - 1)
-        arrive_across(1, step - 1)
-        forward_block(0, step - 1)
+    def forward_step(item, carry):
+        @pl.when(item < ring)
+        def _():
+            way, step = gathered(item)
+            arrive(way, step, step < half - way)
+
+        @pl.when(item < ring + 2)
+        def _():
+            arrive_across(*gathered(item - 2))
+
+        @pl.when(item > 3)
+        def _():
+            forward_block(item - 3)
+
         return carry
 
-    lax.fori_loop(2, half, forward_step, 0)
-    arrive(0, half, False)
-    arrive_across(0, half - 1)
-    if half > 2:
-        forward_block(1, half - 2)
-    arrive_across(1, half - 1)
-    forward_block(0, half - 1)
-    arrive_across(0, half)
-    forward_block(1, half - 1)
-    forward_block(0, half)
+    lax.fori_loop(3, ring + 3, forward_step, 0)
 
     do_copy.wait_recv()
     turn(do_rows, do_cols)
@@ -395,11 +393,11 @@
     att_copy.start()
     att_own[own_heads, :] = att_rows[own_heads, :]
 
-    def backward_tile(way, step, came, zz, xx, first_col):
+    def backward_tile(way, step, zz, xx, first_col):
         span = slice(first_col, 4 * TOK)
         block = rows((zz * 2 + xx) * 2 * TOK, 2 * TOK)
-        out = slice(xx * 2 * TOK, (xx + 1) * 2 * TOK)
-        probs = jnp.exp2(kept_scores[came, step, out, span] - top[:, span])
+        out = rows(xx * 2 * TOK, 2 * TOK)
+        probs = jnp.exp2(kept_scores[1 - way, step, out, span] - top[:, span])
         grad_prob = dot(kv[block, HD:], do_cols[:, span])
         grad_score = (probs * (grad_prob - delta[:, span]) * scale).astype(BF16)
         part[way, step, out, HD:] = dot(probs.astype(BF16), do_rows[span, :])
@@ -415,20 +413,22 @@
             other_core,
         )
 
-    def backward_block(way, step, came=None):
+    def leaving(item):
+        return lax.rem(item, 2), half - lax.div(item + 1, 2)
+
+    def backward_block(item):
+        way, step = leaving(item)
         zz = place(1 - way, step)
-        came = 1 - way if came is None else came
-
-        @pl.when(zz < z)
-        def _():
-            backward_tile(way, step, came, zz, 0, 0)
-            backward_tile(way, step, came, zz, 1, 2 * TOK)
+
+        @pl.when(zz <= z)
+        def _():
+            backward_tile(way, step, zz, 0, 0)
 
         @pl.when(zz > z)
         def _():
-            backward_tile(way, step, came, zz, 0, 2 * TOK)
             part[way, step, 2 * TOK :, :] = jnp.zeros((2 * TOK, 2 * HD), F32)
 
+        backward_tile(way, step, zz, jnp.where(zz <= z, 1, 0), 2 * TOK)
         for xx in range(2):
             swap_copy(way, step, xx).start()
 
@@ -460,7 +460,7 @@
             ring_in.at[way, step - 1, group_rows[group]],
             reduce_send.at[way, step, group],
             reduce_recv.at[way, step - 1, group],
-            along[way],
+            along(way),
         )
 
     def reduce_step(way, step, farthest):
@@ -486,32 +486,23 @@
         ).astype(BF16)
         reduce_copy(way, step, 1).start()
 
-    backward_block(0, half, 0)
-    backward_block(1, half - 1)
-    cross_step(0, half)
-    backward_block(0, half - 1)
-    cross_step(1, half - 1)
-    reduce_step(0, half, half)
-
-    def backward_step(count, carry):
-        step = half - count
-        backward_block(1, step)
-        cross_step(0, step + 1)
-        reduce_step(1, step + 1, half - 1)
-        backward_block(0, step)
-        cross_step(1, step)
-        reduce_step(0, step + 1, half)
+    def backward_step(item, carry):
+        @pl.when(item < ring)
+        def _():
+            backward_block(item)
+
+        @pl.when(item >= 1)
+        def _():
+            cross_step(*leaving(item - 1))
+
+        @pl.when(item >= 2)
+        def _():
+            way, step = leaving(item - 2)
+            reduce_step(way, step, half - way)
+
         return carry
 
-    lax.fori_loop(2, half, backward_step, 0)
-    backward_tile(0, 0, 0, z, 0, 0)
-    backward_tile(0, 0, 0, z, 1, 2 * TOK)
-    for xx in range(2):
-        swap_copy(0, 0, xx).start()
-    cross_step(0, 1)
-    reduce_step(1, 1, half - 1)
-    cross_step(0, 0)
-    reduce_step(0, 1, half)
+    lax.fori_loop(0, ring + 1, backward_step, 0)
 
     for block in range(4):
         span = slice(block * TOK, (block + 1) * TOK)
@@ -532,7 +523,7 @@
 
     for way in range(2):
         reduce_copy(way, 1, 1).wait_recv()
-    kv_send[...] = (pair_sum(0, 0, 1 - x, 0, CUT) + ring_total(group_rows[1])).astype(BF16)
+    kv_send[...] = (pair_sum(1, 0, 1 - x, 0, CUT) + ring_total(group_rows[1])).astype(BF16)
     dkv_copy = copy_once(DKV_X, kv_send, kv_peer, across)
     dkv_copy.start()
 
@@ -544,13 +535,13 @@
         normed_grad = normed_grad + dot_last(lin_grad, w_query[:, span])
     for way in range(2):
         reduce_copy(way, 1, 0).wait_recv()
-    cross_copy(0, 0).wait_recv()
+    cross_copy(1, 0).wait_recv()
     kv_grad[CUT:, :] = (
-        pair_sum(0, 0, x, CUT, TOK - CUT) + ring_total(slice(CUT, TOK)) + cross_in[0, 0].astype(F32)
+        pair_sum(1, 0, x, CUT, TOK - CUT) + ring_total(slice(CUT, TOK)) + cross_in[1, 0].astype(F32)
     )
     dkv_copy.wait_recv()
     kv_grad[:CUT, :] = (
-        pair_sum(0, 0, x, 0, CUT) + ring_total(slice(0, CUT)) + kv_peer[...].astype(F32)
+        pair_sum(1, 0, x, 0, CUT) + ring_total(slice(0, CUT)) + kv_peer[...].astype(F32)
     )
     key_grad = norm_back(k_lin[...], k_gain[...], kv_grad[:, :HD])
     normed_grad = normed_grad + dot_last(key_grad, w_key[...])
@@ -567,26 +558,33 @@
     for once in (codes_copy, grads_copy, kv_copy, q_copy, do_copy, att_copy, dq_copy, dkv_copy):
         once.wait_send()
 
-    def settle(way, step, gathers):
-        for group in range(2):
-            if gathers:
-                gather_copy(way, step, group, z).wait_send()
-                reduce_copy(way, step, group).wait_send()
-            swap_copy(way, step, group).wait_send()
+    def settle_gather(item, carry):
+        way, step = gathered(item)
         for piece in range(3):
             core_copy(way, step, piece, z, c).wait_send()
         relay_copy(way, step, z, x).wait_send()
+        for piece in range(2):
+            gather_copy(way, step, piece, z).wait_send()
+        return carry
+
+    def settle_reduce(item, carry):
+        way, step = leaving(item)
+        for xx in range(2):
+            swap_copy(way, step, xx).wait_send()
         cross_copy(way, step).wait_send()
 
-    settle(0, 0, False)
-
-    def settle_both(step, carry):
-        settle(0, step, True)
-        settle(1, step, True)
+        @pl.when(step > 0)
+        def _():
+            for group in range(2):
+                reduce_copy(way, step, group).wait_send()
+
         return carry
 
-    lax.fori_loop(1, half, settle_both, 0)
-    settle(0, half, True)
+    lax.fori_loop(1, ring, settle_gather, 0)
+    for piece in range(3):
+        core_copy(0, 0, piece, z, c).wait_send()
+    relay_copy(0, 0, z, x).wait_send()
+    lax.fori_loop(0, ring, settle_reduce, 0)
 
 
 def rope_tables(positions, head_dim):

time: 102 us -> 104 us (1.020)
  Pallas kernels: 96.2 us -> 98 us
    pallas_call x1, Pallas kernels: 96.2 us -> 98 us  [local(): pl.pallas_call(functools.partial(kernel, ring, sections), out_shape=(jax....]
where the time goes in v4:
time: 104 us; the launch traced here: 102 us
  Pallas kernels  98 us (94%)
  local copies, waits for them, and re-layouts  2.26 us (2%)
  other arithmetic  1.06 us (1%)
    pallas_call x1, Pallas kernels, local(): pl.pallas_call(functools.partial(kernel, ring, sections), out_shape=(jax....  98 us
    unnamed x4, local copies, waits for them, and re-layouts  2.26 us

profile of v4, /device:TPU:6, one launch (start us, length us, event | category | flops | bytes accessed | tf_op | source)
XLA Modules:
  0.0 102.0 jit_solution(8724812319389121772)
XLA Ops:
  0.7 0.1 broadcast_multiply_fusion
  0.7 1.0 fusion
  1.7 98.0 %shard_map.113 = (bf16[128,512]{1,0:T(8,128)(2,1)}, bf16[128,512]{1,0:T(8,128)(2,1)}) custom-call(bf16[128,512]{1,0:T(8,128)(2,1)} %bitcast.10, bf16[128,512]{1,0:T(8,128)(2,1)} %start_codes.1, bf16[128,512]{1,0:T(8,128)(2,1)} %bitcast.11, bf16[128,512]{1,0:T(8,128)(2,1)} %loss_grads.1, bf16[512,512]{1,0:T(8,128)(2,1)} %bitcast.8, ...), custom_call_target="tpu_custom_call" | custom-call | tf_op jit(solution)/shard_map/pallas_call | solution.py:614
  99.8 0.0 copy-start
  99.8 1.6 %copy.14 = bf16[1,128,512]{2,1,0:T(8,128)(2,1)} copy(bf16[1,128,512]{2,1,0:T(8,128)(2,1)} %bitcast.15) | data formatting | bytes 262144
  101.4 0.0 copy-done
  101.4 0.7 copy.15
  (2 shorter events, 0.0 us)
Async XLA Ops:
  99.8 1.6 %copy-start = (bf16[128,512]{1,0:T(8,128)(2,1)S(1)}, bf16[128,512]{1,0:T(8,128)(2,1)}, u32[]{:S(2)}) copy-start(bf16[128,512]{1,0:T(8,128)(2,1)} %get-tuple-element.5) | copy-start | bytes 393220

commit v5 on v4

v5 whole, which is shorter than its diff:
```python
import functools

import jax
import jax.numpy as jnp
from jax import lax
from jax.experimental import pallas as pl
from jax.experimental.pallas import tpu as pltpu
from jax.sharding import PartitionSpec as P

D = 5120
ROPE_BASE = 1000000.0
NORM_EPS = 1e-06
MASK_FILL = -1e30
LOG2_E = 1.4426950408889634
MESH = pl.DeviceIdType.MESH
F32 = jnp.float32
BF16 = jnp.bfloat16
TOK = 128
HD = 128
PIECE = 64
CONTRACT_LAST = (((1,), (1,)), ((), ()))
CONTRACT_FIRST = (((0,), (0,)), ((), ()))

CODES, GRADS, KV_X, ATT_X, DQ_X, DKV_X, ACC_C, STATS_C, DQ_C0, DQ_C1 = range(10)
Q_X, Q_C, Q_R, DO_X, DO_C, DO_R = range(10, 16)


def dot(a, b):
    return jnp.dot(a, b, preferred_element_type=F32)


def dot_last(a, b):
    return lax.dot_general(a, b, CONTRACT_LAST, preferred_element_type=F32)


def dot_first(a, b):
    return lax.dot_general(a, b, CONTRACT_FIRST, preferred_element_type=F32)


def rows(start, count=TOK):
    return pl.ds(pl.multiple_of(start, TOK), count)


def kernel(
    ring,
    sections,
    sent_codes,
    start_codes,
    sent_grads,
    loss_grads,
    w_query_hbm,
    w_key_hbm,
    w_value_hbm,
    w_out_hbm,
    q_gain,
    k_gain,
    cosines,
    sines,
    out_codes,
    in_grads,
    w_query,
    w_key,
    w_value,
    w_out,
    codes_edge,
    grads_edge,
    codes_buf,
    grads_buf,
    codes_in,
    grads_in,
    q_lin,
    k_lin,
    q_own,
    q_rows,
    q_cols,
    do_own,
    do_rows,
    do_cols,
    kv,
    stats,
    stats_peer,
    acc,
    acc_peer,
    lse,
    delta,
    att_cols,
    att_rows,
    att_own,
    dq_cols,
    dq_rows,
    dq_core,
    dq_out,
    dq_own,
    kept_scores,
    part,
    ring_out,
    ring_in,
    cross_out,
    cross_in,
    kv_grad,
    kv_send,
    kv_peer,
    once_send,
    once_recv,
    gather_send,
    gather_recv,
    reduce_send,
    reduce_recv,
    relay_send,
    relay_recv,
    cross_send,
    cross_recv,
    load_sems,
):
    half = ring // 2
    sec = lax.axis_index("section")
    me = lax.axis_index("seq")
    x = lax.div(me, 2 * ring)
    z = lax.rem(lax.div(me, 2), ring)
    c = lax.rem(me, 2)

    def device(xx, zz, cc):
        return (sec, (xx * ring + zz) * 2 + cc)

    def along(way):
        return device(x, lax.rem(z + 1 + way * (ring - 2), ring), c)

    other_core = device(x, z, 1 - c)
    across = device(1 - x, z, c)
    next_section = (lax.rem(sec + 1, sections), me)
    last_section = (lax.rem(sec + sections - 1, sections), me)

    def copy(src, dst, send, recv, target):
        return pltpu.make_async_remote_copy(
            src_ref=src,
            dst_ref=dst,
            send_sem=send,
            recv_sem=recv,
            device_id=target,
            device_id_type=MESH,
        )

    def copy_once(number, src, dst, target):
        return copy(src, dst, once_send.at[number], once_recv.at[number], target)

    loads = [
        pltpu.make_async_copy(src, dst, load_sems.at[number])
        for number, (src, dst) in enumerate(
            (
                (start_codes, codes_edge),
                (w_key_hbm, w_key),
                (w_value_hbm, w_value),
                (w_query_hbm, w_query),
                (loss_grads, grads_edge),
                (w_out_hbm, w_out),
            )
        )
    ]
    for load in loads:
        load.start()

    barrier = pltpu.get_barrier_semaphore()
    for partner in (along(0), along(1), other_core, across, next_section, last_section):
        pl.semaphore_signal(barrier, inc=1, device_id=partner, device_id_type=MESH)
    pl.semaphore_wait(barrier, 6)

    codes_copy = copy_once(CODES, sent_codes, codes_buf, next_section)
    grads_copy = copy_once(GRADS, sent_grads, grads_buf, last_section)
    codes_copy.start()

    stats[...] = jnp.where(
        lax.broadcasted_iota(jnp.int32, stats.shape, 0) == 0, F32(MASK_FILL), F32(0.0)
    )
    acc[...] = jnp.zeros(acc.shape, F32)
    dq_cols[...] = jnp.zeros(dq_cols.shape, F32)
    for way, farthest in ((0, half), (1, half - 1)):
        ring_in[way, farthest] = jnp.zeros(ring_in.shape[2:], BF16)

    lane = lax.broadcasted_iota(jnp.int32, (TOK, HD), 1)
    first_half = lane < HD // 2
    cos = cosines[...]
    sin = sines[...]
    sin_turned = jnp.where(first_half, -sin, sin)

    def head_norm(tensor, gain):
        inv = lax.rsqrt(jnp.mean(tensor * tensor, axis=-1, keepdims=True) + NORM_EPS)
        hat = tensor * inv * gain
        return (hat * cos + pltpu.roll(hat, HD // 2, 1) * sin_turned).astype(BF16)

    def norm_back(tensor, gain, rot_grad):
        turned = pltpu.roll(rot_grad * sin, HD // 2, 1)
        hat_grad = rot_grad * cos + jnp.where(first_half, turned, -turned)
        inv = lax.rsqrt(jnp.mean(tensor * tensor, axis=-1, keepdims=True) + NORM_EPS)
        scaled = hat_grad * gain
        inner = jnp.mean(tensor * scaled, axis=-1, keepdims=True)
        return (inv * scaled - tensor * (inv * inv * inv) * inner).astype(BF16)

    def piece_of(piece, zz, xx=None):
        if xx is None:
            xx = x if piece < 2 else 1 - x
        start = (zz * 2 + xx) * TOK + piece % 2 * PIECE
        return kv.at[pl.ds(pl.multiple_of(start, PIECE), PIECE)]

    def place(way, step):
        return lax.rem(z + way * step + (1 - way) * (ring - step), ring)

    def gather_copy(way, step, piece, zz):
        ref = piece_of(piece, zz)
        sems = (gather_send.at[way, step, piece], gather_recv.at[way, step, piece])
        return copy(ref, ref, *sems, along(way))

    def relay_copy(way, step, zz, xx):
        ref = piece_of(3, zz, xx)
        return copy(ref, ref, relay_send.at[way, step], relay_recv.at[way, step], across)

    peer_heads = rows((1 - x) * 2 * TOK, 2 * TOK)
    own_heads = rows(x * 2 * TOK, 2 * TOK)
    own_rows = rows((x * 2 + c) * 2 * TOK, 2 * TOK)
    relay_rows = rows(((1 - x) * 2 + c) * 2 * TOK, 2 * TOK)

    def spread(number, src, dst):
        return (
            copy_once(number, src.at[peer_heads], dst.at[own_rows], across),
            copy_once(number + 1, src.at[own_heads], dst.at[own_rows], other_core),
            copy_once(number + 2, dst.at[relay_rows], dst.at[relay_rows], other_core),
        )

    q_copies = spread(Q_X, q_own, q_rows)
    do_copies = spread(DO_X, do_own, do_rows)

    def turn(src, dst):
        for block in range(src.shape[0] // TOK):
            span = slice(block * TOK, (block + 1) * TOK)
            dst[:, span] = src[span, :].T

    for load in loads[:3]:
        load.wait()
    codes_copy.wait_recv()

    @pl.when(sec == 0)
    def _():
        codes_in[...] = codes_edge[...]

    @pl.when(sec != 0)
    def _():
        codes_in[...] = codes_buf[...]

    wide = codes_in[...].astype(F32)
    inv_norm = lax.rsqrt(jnp.sum(wide * wide, axis=-1, keepdims=True) / D + NORM_EPS)
    normed = (wide * inv_norm).astype(BF16)
    key_lin = dot(normed, w_key[...])
    k_lin[...] = key_lin
    own = rows((z * 2 + x) * TOK)
    kv[own, :HD] = head_norm(key_lin, k_gain[...])
    kv[own, HD:] = dot(normed, w_value[...]).astype(BF16)

    first_piece = piece_of(0, z, x)
    kv_copy = copy_once(KV_X, first_piece, first_piece, across)
    kv_copy.start()
    relay_copy(0, 0, z, x).start()
    for piece in (1, 0):
        for way in range(2):
            gather_copy(way, 1, piece, z).start()

    loads[3].wait()
    q_lin[...] = dot(normed, w_query[...])
    for head in range(4):
        q_own[head * TOK : (head + 1) * TOK, :] = head_norm(
            q_lin[:, head * HD : (head + 1) * HD], q_gain[...]
        )
    q_copies[0].start()
    q_copies[1].start()
    q_rows[own_rows, :] = q_own[own_heads, :]

    kv_copy.wait_recv()
    for way in range(2):
        gather_copy(way, 1, 2, z).start()
    grads_copy.start()
    q_copies[0].wait_recv()
    q_copies[2].start()

    scale = HD ** (-0.5)
    scale_two = scale * LOG2_E
    all_cols = 8 * TOK
    late = 4 * TOK

    def own_mask(first_col):
        shape = (TOK, all_cols - first_col)
        key = lax.broadcasted_iota(jnp.int32, shape, 0) + c * TOK
        col = lax.broadcasted_iota(jnp.int32, shape, 1) + first_col
        query = (col & (TOK - 1)) + ((col & (2 * TOK)) >> 1)
        visible = key <= query
        if first_col == 0:
            visible = visible | (col >= late)
        return visible

    def forward_tile(kept, step, zz, xx, first_col, masked):
        span = slice(first_col, all_cols)
        block = rows((zz * 2 + xx) * TOK)
        scores = dot(kv[block, :HD], q_cols[:, span]) * scale_two
        if masked:
            scores = jnp.where(own_mask(first_col), scores, 2 * MASK_FILL)
        kept_scores[kept, step, rows(xx * TOK), span] = scores
        top_old = stats[0:1, span]
        top_new = jnp.maximum(top_old, jnp.max(scores, axis=0, keepdims=True))
        weights = jnp.exp2(scores - top_new)
        shrink = jnp.exp2(top_old - top_new)
        stats[1:2, span] = stats[1:2, span] * shrink + jnp.sum(weights, axis=0, keepdims=True)
        acc[:, span] = acc[:, span] * shrink + dot_first(kv[block, HD:], weights.astype(BF16))
        stats[0:1, span] = top_new

    def arrive(way, step, forward):
        zz = place(way, step)
        for piece in (1, 0, 2):
            gather_copy(way, step, piece, zz).wait_recv()

            @pl.when(forward)
            def _():
                gather_copy(way, step + 1, piece, zz).start()

            if piece == 1:
                relay_copy(way, step, zz, x).start()

    def gathered(item):
        return lax.rem(item + 1, 2), lax.div(item + 1, 2)

    def forward_block(item):
        way, step = gathered(item)
        zz = place(way, step)
        relay_copy(way, step, zz, 1 - x).wait_recv()
        kept = way + lax.div(step, half)

        @pl.when(zz < z)
        def _():
            forward_tile(kept, step, zz, 0, 0, False)
            forward_tile(kept, step, zz, 1, late, False)

        @pl.when(zz > z)
        def _():
            forward_tile(kept, step, zz, 0, late, False)

    arrive(0, 1, half > 1)
    arrive(1, 1, half > 2)
    q_copies[1].wait_recv()
    q_copies[2].wait_recv()
    turn(q_rows, q_cols)
    relay_copy(0, 0, z, 1 - x).wait_recv()
    forward_tile(0, 0, z, 0, 0, True)
    forward_tile(0, 0, z, 1, late, True)

    def forward_step(item, carry):
        @pl.when(item < ring)
        def _():
            way, step = gathered(item)
            arrive(way, step, step < half - way)

        forward_block(item - 2)

        @pl.when(item == 3 + ring // 4)
        def _():
            for load in loads[4:]:
                load.wait()
            grads_copy.wait_recv()

            @pl.when(sec == sections - 1)
            def _():
                grads_in[...] = grads_edge[...]

            @pl.when(sec != sections - 1)
            def _():
                grads_in[...] = grads_buf[...]

            grad_att = dot_last(grads_in[...], w_out[...]).astype(BF16)
            for head in range(4):
                do_own[head * TOK : (head + 1) * TOK, :] = grad_att[:, head * HD : (head + 1) * HD]
            do_copies[0].start()
            do_copies[1].start()
            do_rows[own_rows, :] = do_own[own_heads, :]

        @pl.when(item == 3 + ring // 2)
        def _():
            do_copies[0].wait_recv()
            do_copies[2].start()

        return carry

    lax.fori_loop(3, ring + 2, forward_step, 0)

    acc_copy = copy_once(ACC_C, acc, acc_peer, other_core)
    stats_copy = copy_once(STATS_C, stats, stats_peer, other_core)
    stats_copy.start()
    acc_copy.start()
    do_copies[1].wait_recv()
    do_copies[2].wait_recv()
    turn(do_rows, do_cols)
    stats_copy.wait_recv()
    top = jnp.maximum(stats[0:1, :], stats_peer[0:1, :])
    shrink = jnp.exp2(stats[0:1, :] - top)
    shrink_peer = jnp.exp2(stats_peer[0:1, :] - top)
    total = stats[1:2, :] * shrink + stats_peer[1:2, :] * shrink_peer
    lse[...] = top + jnp.log2(total)
    acc_copy.wait_recv()
    attended = ((acc[...] * shrink + acc_peer[...] * shrink_peer) / total).astype(BF16)
    delta[...] = jnp.sum(
        do_cols[...].astype(F32) * attended.astype(F32), axis=0, keepdims=True
    )
    att_cols[...] = attended

    def backward_tile(way, step, zz, xx, first_col):
        span = slice(first_col, all_cols)
        block = rows((zz * 2 + xx) * TOK)
        out = rows(xx * TOK)
        probs = jnp.exp2(kept_scores[1 - way, step, out, span] - lse[:, span])
        grad_prob = dot(kv[block, HD:], do_cols[:, span])
        grad_score = (probs * (grad_prob - delta[:, span]) * scale).astype(BF16)
        part[way, step, out, HD:] = dot(probs.astype(BF16), do_rows[span, :])
        part[way, step, out, :HD] = dot(grad_score, q_rows[span, :])
        dq_cols[:, span] += dot_first(kv[block, :HD], grad_score)

    def leaving(item):
        return lax.rem(item, 2), half - lax.div(item + 1, 2)

    def own_part(way, step, piece):
        xx = x if piece < 2 else 1 - x
        return part[way, step, pl.ds(pl.multiple_of(xx * TOK + piece % 2 * PIECE, PIECE), PIECE), :]

    def cross_copy(way, step):
        return copy(
            cross_out.at[way, step],
            cross_in.at[way, step],
            cross_send.at[way, step],
            cross_recv.at[way, step],
            across,
        )

    def backward_block(item):
        way, step = leaving(item)
        zz = place(1 - way, step)

        @pl.when(zz <= z)
        def _():
            backward_tile(way, step, zz, 0, 0)
            backward_tile(way, step, zz, 1, late)

        @pl.when(zz > z)
        def _():
            backward_tile(way, step, zz, 0, late)
            part[way, step, TOK:, :] = jnp.zeros((TOK, 2 * HD), F32)

        cross_out[way, step] = own_part(way, step, 3).astype(BF16)
        cross_copy(way, step).start()

    def reduce_copy(way, step, piece):
        span = slice(piece * PIECE, (piece + 1) * PIECE)
        return copy(
            ring_out.at[way, step, span],
            ring_in.at[way, step - 1, span],
            reduce_send.at[way, step, piece],
            reduce_recv.at[way, step - 1, piece],
            along(way),
        )

    def reduce_step(item):
        way, step = leaving(item)
        for piece in (0, 2, 1):

            @pl.when(step < half - way)
            def _():
                reduce_copy(way, step + 1, piece).wait_recv()

            span = slice(piece * PIECE, (piece + 1) * PIECE)
            summed = own_part(way, step, piece) + ring_in[way, step, span].astype(F32)
            if piece == 1:
                cross_copy(way, step).wait_recv()
                summed = summed + cross_in[way, step].astype(F32)
            ring_out[way, step, span] = summed.astype(BF16)
            reduce_copy(way, step, piece).start()

    def backward_step(pair, carry):
        backward_block(2 * pair)
        backward_block(2 * pair + 1)

        @pl.when(pair > 0)
        def _():
            reduce_step(pair - 1)

        return carry

    def reduce_only(item, carry):
        reduce_step(item)
        return carry

    lax.fori_loop(0, half, backward_step, 0)

    turn_back = [(xx, head) for xx in range(2) for head in range(2)]
    for block in range(8):
        span = slice(block * TOK, (block + 1) * TOK)
        dq_rows[span, :] = dq_cols[:, span].T
    dq_core_copies = [
        copy_once(
            number,
            dq_rows.at[rows((xx * 2 + 1 - c) * 2 * TOK, 2 * TOK)],
            dq_core.at[rows(xx * 2 * TOK, 2 * TOK)],
            other_core,
        )
        for xx, number in enumerate((DQ_C0, DQ_C1))
    ]
    for number in range(2):
        dq_core_copies[number].start()
    reduce_step(half - 1)

    for number in range(2):
        dq_core_copies[number].wait_recv()
    dq_out[...] = dq_rows[relay_rows, :] + dq_core[peer_heads, :]
    dq_copy = copy_once(DQ_X, dq_out, dq_own.at[own_heads], across)
    dq_copy.start()
    dq_own[own_heads, :] = dq_rows[own_rows, :] + dq_core[own_heads, :]

    for xx, head in turn_back:
        cols = rows(((xx * 2 + c) * 2 + head) * TOK)
        att_rows[(xx * 2 + head) * TOK : (xx * 2 + head + 1) * TOK, :] = att_cols[:, cols].T
    att_copy = copy_once(ATT_X, att_rows.at[peer_heads], att_own.at[own_heads], across)
    att_copy.start()
    att_own[own_heads, :] = att_rows[own_heads, :]

    lax.fori_loop(half, ring - 1, reduce_only, 0)

    att_copy.wait_recv()
    result = codes_in[...].astype(F32)
    for head in range(4):
        span = slice(head * TOK, (head + 1) * TOK)
        result = result + dot(att_own[span, :], w_out[span, :])
    out_codes[...] = result.astype(BF16)

    dq_copy.wait_recv()
    normed_grad = jnp.zeros((TOK, w_query.shape[0]), F32)
    for head in range(4):
        span = slice(head * TOK, (head + 1) * TOK)
        lin_grad = norm_back(q_lin[:, span], q_gain[...], dq_own[span, :])
        normed_grad = normed_grad + dot_last(lin_grad, w_query[:, span])

    def own_total(piece):
        for way in range(2):
            reduce_copy(way, 1, piece).wait_recv()
        span = slice(piece * PIECE, (piece + 1) * PIECE)
        ringed = ring_in[0, 0, span].astype(F32) + ring_in[1, 0, span].astype(F32)
        return own_part(1, 0, piece) + ringed

    kv_send[...] = own_total(2).astype(BF16)
    dkv_copy = copy_once(DKV_X, kv_send, kv_peer, across)
    dkv_copy.start()

    cross_copy(1, 0).wait_recv()
    kv_grad[PIECE:, :] = own_total(1) + cross_in[1, 0].astype(F32)
    first_total = own_total(0)
    dkv_copy.wait_recv()
    kv_grad[:PIECE, :] = first_total + kv_peer[...].astype(F32)
    key_grad = norm_back(k_lin[...], k_gain[...], kv_grad[:, :HD])
    normed_grad = normed_grad + dot_last(key_grad, w_key[...])
    normed_grad = normed_grad + dot_last(kv_grad[:, HD:].astype(BF16), w_value[...])
    wide = codes_in[...].astype(F32)
    inv_norm = lax.rsqrt(jnp.sum(wide * wide, axis=-1, keepdims=True) / D + NORM_EPS)
    inner = jnp.sum(wide * normed_grad, axis=-1, keepdims=True)
    in_grads[...] = (
        grads_in[...].astype(F32)
        + inv_norm * normed_grad
        - wide * (inv_norm * inv_norm * inv_norm) * inner / D
    ).astype(BF16)

    for once in (codes_copy, grads_copy, kv_copy, acc_copy, stats_copy, att_copy, dq_copy, dkv_copy):
        once.wait_send()
    for once in (*q_copies, *do_copies, *dq_core_copies):
        once.wait_send()

    def settle_gather(item, carry):
        way, step = gathered(item)
        relay_copy(way, step, z, x).wait_send()
        for piece in range(3):
            gather_copy(way, step, piece, z).wait_send()
        return carry

    def settle_reduce(item, carry):
        way, step = leaving(item)
        cross_copy(way, step).wait_send()

        @pl.when(step > 0)
        def _():
            for piece in range(3):
                reduce_copy(way, step, piece).wait_send()

        return carry

    lax.fori_loop(1, ring, settle_gather, 0)
    relay_copy(0, 0, z, x).wait_send()
    lax.fori_loop(0, ring, settle_reduce, 0)


def rope_tables(positions, head_dim):
    half_dim = head_dim // 2
    exponent = jnp.arange(half_dim).astype(F32) * (2.0 / head_dim)
    frequency = jnp.power(F32(ROPE_BASE), -exponent)
    angles = positions.astype(F32)[:, None] * frequency[None, :]
    angles = jnp.concatenate([angles, angles], axis=-1)
    return (jnp.cos(angles), jnp.sin(angles))


def local(
    sent_codes, start_codes, sent_grads, loss_grads, w_query, w_key, w_value, w_out, q_gain, k_gain
):
    ring = lax.axis_size("seq") // 4
    sections = lax.axis_size("section")
    steps = ring // 2 + 1
    width = start_codes.shape[1]
    positions = lax.axis_index("seq") * TOK + jnp.arange(TOK, dtype=jnp.int32)
    cosines, sines = rope_tables(positions, HD)
    vmem = pltpu.VMEM
    dma = pltpu.SemaphoreType.DMA
    one_block = (TOK, width)
    heads = (4 * TOK, HD)
    all_rows = (8 * TOK, HD)
    columns = (HD, 8 * TOK)
    stat = (1, 8 * TOK)
    results = pl.pallas_call(
        functools.partial(kernel, ring, sections),
        out_shape=(jax.ShapeDtypeStruct(one_block, BF16),) * 2,
        in_specs=[pl.BlockSpec(memory_space=pltpu.HBM)] * 8 + [pl.BlockSpec(memory_space=vmem)] * 4,
        out_specs=(pl.BlockSpec(memory_space=vmem),) * 2,
        scratch_shapes=[
            vmem(w_query.shape[1:], BF16),
            vmem(w_key.shape[1:], BF16),
            vmem(w_value.shape[1:], BF16),
            vmem(w_out.shape[1:], BF16),
            vmem(one_block, BF16),
            vmem(one_block, BF16),
            vmem(one_block, BF16),
            vmem(one_block, BF16),
            vmem(one_block, BF16),
            vmem(one_block, BF16),
            vmem(one_block, F32),
            vmem((TOK, HD), F32),
            vmem(heads, BF16),
            vmem(all_rows, BF16),
            vmem(columns, BF16),
            vmem(heads, BF16),
            vmem(all_rows, BF16),
            vmem(columns, BF16),
            vmem((ring * 2 * TOK, 2 * HD), BF16),
            vmem((8, 8 * TOK), F32),
            vmem((8, 8 * TOK), F32),
            vmem(columns, F32),
            vmem(columns, F32),
            vmem(stat, F32),
            vmem(stat, F32),
            vmem(columns, BF16),
            vmem(heads, BF16),
            vmem(heads, BF16),
            vmem(columns, F32),
            vmem(all_rows, F32),
            vmem(heads, F32),
            vmem((2 * TOK, HD), F32),
            vmem(heads, F32),
            vmem((2, steps, 2 * TOK, 8 * TOK), F32),
            vmem((2, steps, 2 * TOK, 2 * HD), F32),
            vmem((2, steps, 3 * PIECE, 2 * HD), BF16),
            vmem((2, steps, 3 * PIECE, 2 * HD), BF16),
            vmem((2, steps, PIECE, 2 * HD), BF16),
            vmem((2, steps, PIECE, 2 * HD), BF16),
            vmem((TOK, 2 * HD), F32),
            vmem((PIECE, 2 * HD), BF16),
            vmem((PIECE, 2 * HD), BF16),
            dma((16,)),
            dma((16,)),
            dma((2, steps, 3)),
            dma((2, steps, 3)),
            dma((2, steps, 3)),
            dma((2, steps, 3)),
            dma((2, steps)),
            dma((2, steps)),
            dma((2, steps)),
            dma((2, steps)),
            dma((6,)),
        ],
        compiler_params=pltpu.CompilerParams(
            collective_id=0, has_side_effects=True, vmem_limit_bytes=60 * 1024 * 1024
        ),
    )(
        sent_codes[0],
        start_codes,
        sent_grads[0],
        loss_grads,
        w_query[0],
        w_key[0],
        w_value[0],
        w_out[0],
        q_gain,
        k_gain,
        cosines,
        sines,
    )
    return (results[0][None], results[1][None])


def solution(mesh):
    in_specs = (
        P("section", "seq", None),
        P("seq", None),
        P("section", "seq", None),
        P("seq", None),
        P("section", None, None),
        P("section", None, None),
        P("section", None, None),
        P("section", None, None),
        P("section", None),
        P("section", None),
    )
    out_specs = (P("section", "seq", None), P("section", "seq", None))
    return jax.shard_map(local, mesh=mesh, in_specs=in_specs, out_specs=out_specs, check_vma=False)
```

time: 104 us -> 97.7 us (0.939); the launches traced: 102 us -> 96.9 us
  Pallas kernels: 98 us -> 92.9 us
    pallas_call x1, Pallas kernels: 98 us -> 92.9 us  [local(): pl.pallas_call(functools.partial(kernel, ring, sections), out_shape=(jax....]
where the time goes in v5:
time: 97.7 us; the launch traced here: 96.9 us
  Pallas kernels  92.9 us (95%)
  local copies, waits for them, and re-layouts  2.26 us (2%)
  other arithmetic  1.06 us (1%)
    pallas_call x1, Pallas kernels, local(): pl.pallas_call(functools.partial(kernel, ring, sections), out_shape=(jax....  92.9 us
    unnamed x4, local copies, waits for them, and re-layouts  2.26 us

profile of v5, /device:TPU:6, one launch (start us, length us, event | category | flops | bytes accessed | tf_op | source)
XLA Modules:
  0.0 96.9 jit_solution(9779242334793750434)
XLA Ops:
  0.7 0.1 broadcast_multiply_fusion
  0.7 1.0 %fusion = (f32[128,128]{1,0:T(8,128)}, f32[128,128]{1,0:T(8,128)}) fusion(f32[128,64]{1,0:T(8,128)S(1)} %broadcast_multiply_fusion), kind=kLoop, calls=%fused_computation.1 | loop fusion | flops 16384 | bytes 163840 | tf_op jit(solution)/shard_map/sin | solution.py:604
  1.7 92.9 %shard_map.113 = (bf16[128,512]{1,0:T(8,128)(2,1)}, bf16[128,512]{1,0:T(8,128)(2,1)}) custom-call(bf16[128,512]{1,0:T(8,128)(2,1)} %bitcast.10, bf16[128,512]{1,0:T(8,128)(2,1)} %start_codes.1, bf16[128,512]{1,0:T(8,128)(2,1)} %bitcast.11, bf16[128,512]{1,0:T(8,128)(2,1)} %loss_grads.1, bf16[512,512]{1,0:T(8,128)(2,1)} %bitcast.8, ...), custom_call_target="tpu_custom_call" | custom-call | tf_op jit(solution)/shard_map/pallas_call | solution.py:623
  94.6 0.0 copy-start
  94.6 1.6 %copy.14 = bf16[1,128,512]{2,1,0:T(8,128)(2,1)} copy(bf16[1,128,512]{2,1,0:T(8,128)(2,1)} %bitcast.15) | data formatting | bytes 262144
  96.2 0.0 copy-done
  96.2 0.7 copy.15
  (2 shorter events, 0.0 us)
Async XLA Ops:
  94.6 1.6 %copy-start = (bf16[128,512]{1,0:T(8,128)(2,1)S(1)}, bf16[128,512]{1,0:T(8,128)(2,1)}, u32[]{:S(2)}) copy-start(bf16[128,512]{1,0:T(8,128)(2,1)} %get-tuple-element.5) | copy-start | bytes 393220

commit v6 on v5

--- a/solution.py
+++ b/solution.py
@@ -125,6 +125,9 @@
     def along(way):
         return device(x, lax.rem(z + 1 + way * (ring - 2), ring), c)
 
+    def diagonal(way):
+        return device(1 - x, lax.rem(z + 1 + way * (ring - 2), ring), c)
+
     other_core = device(x, z, 1 - c)
     across = device(1 - x, z, c)
     next_section = (lax.rem(sec + 1, sections), me)
@@ -160,9 +163,10 @@
         load.start()
 
     barrier = pltpu.get_barrier_semaphore()
-    for partner in (along(0), along(1), other_core, across, next_section, last_section):
+    partners = (along(0), along(1), diagonal(0), diagonal(1), other_core, across)
+    for partner in (*partners, next_section, last_section):
         pl.semaphore_signal(barrier, inc=1, device_id=partner, device_id_type=MESH)
-    pl.semaphore_wait(barrier, 6)
+    pl.semaphore_wait(barrier, 8)
 
     codes_copy = copy_once(CODES, sent_codes, codes_buf, next_section)
     grads_copy = copy_once(GRADS, sent_grads, grads_buf, last_section)
@@ -255,12 +259,15 @@
     kv[own, HD:] = dot(normed, w_value[...]).astype(BF16)
 
     first_piece = piece_of(0, z, x)
+    for piece in (1, 0):
+        for way in range(2):
+            gather_copy(way, 1, piece, z).start()
+    for way in range(2):
+        sems = (gather_send.at[way, 1, 2], gather_recv.at[way, 1, 2])
+        copy(first_piece, first_piece, *sems, diagonal(way)).start()
     kv_copy = copy_once(KV_X, first_piece, first_piece, across)
     kv_copy.start()
     relay_copy(0, 0, z, x).start()
-    for piece in (1, 0):
-        for way in range(2):
-            gather_copy(way, 1, piece, z).start()
 
     loads[3].wait()
     q_lin[...] = dot(normed, w_query[...])
@@ -272,12 +279,7 @@
     q_copies[1].start()
     q_rows[own_rows, :] = q_own[own_heads, :]
 
-    kv_copy.wait_recv()
-    for way in range(2):
-        gather_copy(way, 1, 2, z).start()
     grads_copy.start()
-    q_copies[0].wait_recv()
-    q_copies[2].start()
 
     scale = HD ** (-0.5)
     scale_two = scale * LOG2_E
@@ -339,11 +341,21 @@
         def _():
             forward_tile(kept, step, zz, 0, late, False)
 
-    arrive(0, 1, half > 1)
-    arrive(1, 1, half > 2)
+    def arrive_item(item):
+        way, step = gathered(item)
+        arrive(way, step, step < half - way)
+
+    arrive_item(1)
+    arrive_item(2)
+    q_copies[0].wait_recv()
+    q_copies[2].start()
+    arrive_item(3)
+    if ring > 4:
+        arrive_item(4)
     q_copies[1].wait_recv()
     q_copies[2].wait_recv()
     turn(q_rows, q_cols)
+    kv_copy.wait_recv()
     relay_copy(0, 0, z, 1 - x).wait_recv()
     forward_tile(0, 0, z, 0, 0, True)
     forward_tile(0, 0, z, 1, late, True)
@@ -351,12 +363,11 @@
     def forward_step(item, carry):
         @pl.when(item < ring)
         def _():
-            way, step = gathered(item)
-            arrive(way, step, step < half - way)
-
-        forward_block(item - 2)
-
-        @pl.when(item == 3 + ring // 4)
+            arrive_item(item)
+
+        forward_block(item - 4)
+
+        @pl.when(item == 5 + ring // 4)
         def _():
             for load in loads[4:]:
                 load.wait()
@@ -377,14 +388,14 @@
             do_copies[1].start()
             do_rows[own_rows, :] = do_own[own_heads, :]
 
-        @pl.when(item == 3 + ring // 2)
+        @pl.when(item == 5 + ring // 2)
         def _():
             do_copies[0].wait_recv()
             do_copies[2].start()
 
         return carry
 
-    lax.fori_loop(3, ring + 2, forward_step, 0)
+    lax.fori_loop(5, ring + 4, forward_step, 0)
 
     acc_copy = copy_once(ACC_C, acc, acc_peer, other_core)
     stats_copy = copy_once(STATS_C, stats, stats_peer, other_core)
@@ -400,7 +411,9 @@
     total = stats[1:2, :] * shrink + stats_peer[1:2, :] * shrink_peer
     lse[...] = top + jnp.log2(total)
     acc_copy.wait_recv()
-    attended = ((acc[...] * shrink + acc_peer[...] * shrink_peer) / total).astype(BF16)
+    attended = (
+        acc[...] * (shrink / total) + acc_peer[...] * (shrink_peer / total)
+    ).astype(BF16)
     delta[...] = jnp.sum(
         do_cols[...].astype(F32) * attended.astype(F32), axis=0, keepdims=True
     )
@@ -450,17 +463,17 @@
         cross_out[way, step] = own_part(way, step, 3).astype(BF16)
         cross_copy(way, step).start()
 
-    def reduce_copy(way, step, piece):
+    def reduce_copy(way, step, piece, target=None):
         span = slice(piece * PIECE, (piece + 1) * PIECE)
         return copy(
             ring_out.at[way, step, span],
             ring_in.at[way, step - 1, span],
             reduce_send.at[way, step, piece],
             reduce_recv.at[way, step - 1, piece],
-            along(way),
+            along(way) if target is None else target,
         )
 
-    def reduce_step(item):
+    def reduce_step(item, last=False):
         way, step = leaving(item)
         for piece in (0, 2, 1):
 
@@ -474,7 +487,8 @@
                 cross_copy(way, step).wait_recv()
                 summed = summed + cross_in[way, step].astype(F32)
             ring_out[way, step, span] = summed.astype(BF16)
-            reduce_copy(way, step, piece).start()
+            target = diagonal(way) if last and piece == 2 else None
+            reduce_copy(way, step, piece, target).start()
 
     def backward_step(pair, carry):
         backward_block(2 * pair)
@@ -492,6 +506,9 @@
 
     lax.fori_loop(0, half, backward_step, 0)
 
+    kv_send[...] = own_part(1, 0, 2).astype(BF16)
+    dkv_copy = copy_once(DKV_X, kv_send, kv_peer, across)
+    dkv_copy.start()
     turn_back = [(xx, head) for xx in range(2) for head in range(2)]
     for block in range(8):
         span = slice(block * TOK, (block + 1) * TOK)
@@ -507,8 +524,27 @@
     ]
     for number in range(2):
         dq_core_copies[number].start()
-    reduce_step(half - 1)
-
+    reduce_step(half - 1, half - 1 >= ring - 3)
+
+    def settle_gather(item, carry):
+        way, step = gathered(item)
+        relay_copy(way, step, z, x).wait_send()
+        for piece in range(3):
+            gather_copy(way, step, piece, z).wait_send()
+        return carry
+
+    def settle_reduce(item, carry):
+        way, step = leaving(item)
+        cross_copy(way, step).wait_send()
+
+        @pl.when(step > 0)
+        def _():
+            for piece in range(3):
+                reduce_copy(way, step, piece).wait_send()
+
+        return carry
+
+    lax.fori_loop(1, ring, settle_gather, 0)
     for number in range(2):
         dq_core_copies[number].wait_recv()
     dq_out[...] = dq_rows[relay_rows, :] + dq_core[peer_heads, :]
@@ -523,7 +559,10 @@
     att_copy.start()
     att_own[own_heads, :] = att_rows[own_heads, :]
 
-    lax.fori_loop(half, ring - 1, reduce_only, 0)
+    lax.fori_loop(half, ring - 3, reduce_only, 0)
+    for item in range(max(half, ring - 3), ring - 1):
+        reduce_step(item, True)
+    lax.fori_loop(0, ring - 3, settle_reduce, 0)
 
     att_copy.wait_recv()
     result = codes_in[...].astype(F32)
@@ -539,22 +578,18 @@
         lin_grad = norm_back(q_lin[:, span], q_gain[...], dq_own[span, :])
         normed_grad = normed_grad + dot_last(lin_grad, w_query[:, span])
 
-    def own_total(piece):
+    def ringed(piece):
         for way in range(2):
             reduce_copy(way, 1, piece).wait_recv()
         span = slice(piece * PIECE, (piece + 1) * PIECE)
-        ringed = ring_in[0, 0, span].astype(F32) + ring_in[1, 0, span].astype(F32)
-        return own_part(1, 0, piece) + ringed
-
-    kv_send[...] = own_total(2).astype(BF16)
-    dkv_copy = copy_once(DKV_X, kv_send, kv_peer, across)
-    dkv_copy.start()
+        return ring_in[0, 0, span].astype(F32) + ring_in[1, 0, span].astype(F32)
 
     cross_copy(1, 0).wait_recv()
-    kv_grad[PIECE:, :] = own_total(1) + cross_in[1, 0].astype(F32)
-    first_total = own_total(0)
     dkv_copy.wait_recv()
-    kv_grad[:PIECE, :] = first_total + kv_peer[...].astype(F32)
+    first_part = own_part(1, 0, 0) + kv_peer[...].astype(F32)
+    second_part = own_part(1, 0, 1) + cross_in[1, 0].astype(F32)
+    kv_grad[:PIECE, :] = first_part + ringed(0) + ringed(2)
+    kv_grad[PIECE:, :] = second_part + ringed(1)
     key_grad = norm_back(k_lin[...], k_gain[...], kv_grad[:, :HD])
     normed_grad = normed_grad + dot_last(key_grad, w_key[...])
     normed_grad = normed_grad + dot_last(kv_grad[:, HD:].astype(BF16), w_value[...])
@@ -572,27 +607,8 @@
     for once in (*q_copies, *do_copies, *dq_core_copies):
         once.wait_send()
 
-    def settle_gather(item, carry):
-        way, step = gathered(item)
-        relay_copy(way, step, z, x).wait_send()
-        for piece in range(3):
-            gather_copy(way, step, piece, z).wait_send()
-        return carry
-
-    def settle_reduce(item, carry):
-        way, step = leaving(item)
-        cross_copy(way, step).wait_send()
-
-        @pl.when(step > 0)
-        def _():
-            for piece in range(3):
-                reduce_copy(way, step, piece).wait_send()
-
-        return carry
-
-    lax.fori_loop(1, ring, settle_gather, 0)
     relay_copy(0, 0, z, x).wait_send()
-    lax.fori_loop(0, ring, settle_reduce, 0)
+    lax.fori_loop(ring - 3, ring, settle_reduce, 0)
 
 
 def rope_tables(positions, head_dim):

time: 97.7 us -> 94.5 us (0.967)
  Pallas kernels: 92.9 us -> 90.3 us
    pallas_call x1, Pallas kernels: 92.9 us -> 90.3 us  [local(): pl.pallas_call(functools.partial(kernel, ring, sections), out_shape=(jax....]
where the time goes in v6:
time: 94.5 us; the launch traced here: 94.3 us
  Pallas kernels  90.3 us (96%)
  local copies, waits for them, and re-layouts  2.26 us (2%)
  other arithmetic  1.06 us (1%)
    pallas_call x1, Pallas kernels, local(): pl.pallas_call(functools.partial(kernel, ring, sections), out_shape=(jax....  90.3 us
    unnamed x4, local copies, waits for them, and re-layouts  2.26 us

profile of v6, /device:TPU:6, one launch (start us, length us, event | category | flops | bytes accessed | tf_op | source)
XLA Modules:
  0.0 94.3 jit_solution(13513144004973885805)
XLA Ops:
  0.7 0.1 broadcast_multiply_fusion
  0.7 1.0 %fusion = (f32[128,128]{1,0:T(8,128)}, f32[128,128]{1,0:T(8,128)}) fusion(f32[128,64]{1,0:T(8,128)S(1)} %broadcast_multiply_fusion), kind=kLoop, calls=%fused_computation.1 | loop fusion | flops 16384 | bytes 163840 | tf_op jit(solution)/shard_map/sin | solution.py:620
  1.7 90.3 %shard_map.113 = (bf16[128,512]{1,0:T(8,128)(2,1)}, bf16[128,512]{1,0:T(8,128)(2,1)}) custom-call(bf16[128,512]{1,0:T(8,128)(2,1)} %bitcast.10, bf16[128,512]{1,0:T(8,128)(2,1)} %start_codes.1, bf16[128,512]{1,0:T(8,128)(2,1)} %bitcast.11, bf16[128,512]{1,0:T(8,128)(2,1)} %loss_grads.1, bf16[512,512]{1,0:T(8,128)(2,1)} %bitcast.8, ...), custom_call_target="tpu_custom_call" | custom-call | tf_op jit(solution)/shard_map/pallas_call | solution.py:639
  92.0 0.0 copy-start
  92.0 1.6 %copy.14 = bf16[1,128,512]{2,1,0:T(8,128)(2,1)} copy(bf16[1,128,512]{2,1,0:T(8,128)(2,1)} %bitcast.15) | data formatting | bytes 262144
  93.6 0.0 copy-done
  93.6 0.7 copy.15
  (2 shorter events, 0.0 us)
Async XLA Ops:
  92.0 1.6 %copy-start = (bf16[128,512]{1,0:T(8,128)(2,1)S(1)}, bf16[128,512]{1,0:T(8,128)(2,1)}, u32[]{:S(2)}) copy-start(bf16[128,512]{1,0:T(8,128)(2,1)} %get-tuple-element.5) | copy-start | bytes 393220

commit v7 on v6

--- a/solution.py
+++ b/solution.py
@@ -91,7 +91,8 @@
     dq_core,
     dq_out,
     dq_own,
-    kept_scores,
+    kept_weights,
+    kept_tops,
     part,
     ring_out,
     ring_in,
@@ -182,8 +183,16 @@
 
     lane = lax.broadcasted_iota(jnp.int32, (TOK, HD), 1)
     first_half = lane < HD // 2
-    cos = cosines[...]
-    sin = sines[...]
+
+    def unpack_table(packed):
+        turned = pltpu.roll(packed, HD // 2, 1)
+        left = first_half[: TOK // 2]
+        return jnp.concatenate(
+            [jnp.where(left, packed, turned), jnp.where(left, turned, packed)], axis=0
+        )
+
+    cos = unpack_table(cosines[...])
+    sin = unpack_table(sines[...])
     sin_turned = jnp.where(first_half, -sin, sin)
 
     def head_norm(tensor, gain):
@@ -302,10 +311,11 @@
         scores = dot(kv[block, :HD], q_cols[:, span]) * scale_two
         if masked:
             scores = jnp.where(own_mask(first_col), scores, 2 * MASK_FILL)
-        kept_scores[kept, step, rows(xx * TOK), span] = scores
         top_old = stats[0:1, span]
         top_new = jnp.maximum(top_old, jnp.max(scores, axis=0, keepdims=True))
         weights = jnp.exp2(scores - top_new)
+        kept_weights[kept, step, rows(xx * TOK), span] = weights
+        kept_tops[kept, step, xx : xx + 1, span] = top_new
         shrink = jnp.exp2(top_old - top_new)
         stats[1:2, span] = stats[1:2, span] * shrink + jnp.sum(weights, axis=0, keepdims=True)
         acc[:, span] = acc[:, span] * shrink + dot_first(kv[block, HD:], weights.astype(BF16))
@@ -423,7 +433,8 @@
         span = slice(first_col, all_cols)
         block = rows((zz * 2 + xx) * TOK)
         out = rows(xx * TOK)
-        probs = jnp.exp2(kept_scores[1 - way, step, out, span] - lse[:, span])
+        factor = jnp.exp2(kept_tops[1 - way, step, xx : xx + 1, span] - lse[:, span])
+        probs = kept_weights[1 - way, step, out, span] * factor
         grad_prob = dot(kv[block, HD:], do_cols[:, span])
         grad_score = (probs * (grad_prob - delta[:, span]) * scale).astype(BF16)
         part[way, step, out, HD:] = dot(probs.astype(BF16), do_rows[span, :])
@@ -490,21 +501,27 @@
             target = diagonal(way) if last and piece == 2 else None
             reduce_copy(way, step, piece, target).start()
 
-    def backward_step(pair, carry):
-        backward_block(2 * pair)
-        backward_block(2 * pair + 1)
-
-        @pl.when(pair > 0)
-        def _():
-            reduce_step(pair - 1)
-
+    def backward_step(count, carry):
+        block = 2 + 3 * count
+        backward_block(block)
+        reduce_step(2 * count)
+        backward_block(block + 1)
+        reduce_step(2 * count + 1)
+        backward_block(block + 2)
         return carry
 
     def reduce_only(item, carry):
         reduce_step(item)
         return carry
 
-    lax.fori_loop(0, half, backward_step, 0)
+    rounds = (ring - 4) // 3
+    reduced = 2 * rounds
+    backward_block(0)
+    backward_block(1)
+    lax.fori_loop(0, rounds, backward_step, 0)
+    backward_block(ring - 2)
+    reduce_step(reduced)
+    backward_block(ring - 1)
 
     kv_send[...] = own_part(1, 0, 2).astype(BF16)
     dkv_copy = copy_once(DKV_X, kv_send, kv_peer, across)
@@ -524,7 +541,7 @@
     ]
     for number in range(2):
         dq_core_copies[number].start()
-    reduce_step(half - 1, half - 1 >= ring - 3)
+    reduce_step(reduced + 1, reduced + 1 >= ring - 3)
 
     def settle_gather(item, carry):
         way, step = gathered(item)
@@ -559,8 +576,8 @@
     att_copy.start()
     att_own[own_heads, :] = att_rows[own_heads, :]
 
-    lax.fori_loop(half, ring - 3, reduce_only, 0)
-    for item in range(max(half, ring - 3), ring - 1):
+    lax.fori_loop(reduced + 2, ring - 3, reduce_only, 0)
+    for item in range(max(reduced + 2, ring - 3), ring - 1):
         reduce_step(item, True)
     lax.fori_loop(0, ring - 3, settle_reduce, 0)
 
@@ -611,12 +628,15 @@
     lax.fori_loop(ring - 3, ring, settle_reduce, 0)
 
 
-def rope_tables(positions, head_dim):
-    half_dim = head_dim // 2
-    exponent = jnp.arange(half_dim).astype(F32) * (2.0 / head_dim)
+def rope_tables(first_pos):
+    half_dim = HD // 2
+    exponent = jnp.arange(half_dim).astype(F32) * (2.0 / HD)
     frequency = jnp.power(F32(ROPE_BASE), -exponent)
-    angles = positions.astype(F32)[:, None] * frequency[None, :]
-    angles = jnp.concatenate([angles, angles], axis=-1)
+    frequency = jnp.concatenate([frequency, frequency])
+    shape = (TOK // 2, HD)
+    lane = lax.broadcasted_iota(jnp.int32, shape, 1)
+    offset = lax.broadcasted_iota(jnp.int32, shape, 0) + jnp.where(lane < half_dim, 0, TOK // 2)
+    angles = (first_pos + offset).astype(F32) * frequency[None, :]
     return (jnp.cos(angles), jnp.sin(angles))
 
 
@@ -627,8 +647,7 @@
     sections = lax.axis_size("section")
     steps = ring // 2 + 1
     width = start_codes.shape[1]
-    positions = lax.axis_index("seq") * TOK + jnp.arange(TOK, dtype=jnp.int32)
-    cosines, sines = rope_tables(positions, HD)
+    cosines, sines = rope_tables(lax.axis_index("seq") * TOK)
     vmem = pltpu.VMEM
     dma = pltpu.SemaphoreType.DMA
     one_block = (TOK, width)
@@ -676,6 +695,7 @@
             vmem((2 * TOK, HD), F32),
             vmem(heads, F32),
             vmem((2, steps, 2 * TOK, 8 * TOK), F32),
+            vmem((2, steps, 8, 8 * TOK), F32),
             vmem((2, steps, 2 * TOK, 2 * HD), F32),
             vmem((2, steps, 3 * PIECE, 2 * HD), BF16),
             vmem((2, steps, 3 * PIECE, 2 * HD), BF16),

time: 94.5 us -> 92.4 us (0.978)
  Pallas kernels: 90.3 us -> 87.9 us
    pallas_call x1, Pallas kernels: 90.3 us -> 87.9 us  [local(): pl.pallas_call(functools.partial(kernel, ring, sections), out_shape=(jax....]
where the time goes in v7:
time: 92.4 us; the launch traced here: 91.6 us
  Pallas kernels  87.9 us (95%)
  local copies, waits for them, and re-layouts  2.26 us (2%)
    pallas_call x1, Pallas kernels, local(): pl.pallas_call(functools.partial(kernel, ring, sections), out_shape=(jax....  87.9 us
    unnamed x4, local copies, waits for them, and re-layouts  2.26 us

profile of v7, /device:TPU:6, one launch (start us, length us, event | category | flops | bytes accessed | tf_op | source)
XLA Modules:
  0.0 91.6 jit_solution(3936798609310216871)
XLA Ops:
  0.6 0.1 pad_maximum_fusion
  0.7 0.8 fusion
  1.5 87.9 %shard_map.113 = (bf16[128,512]{1,0:T(8,128)(2,1)}, bf16[128,512]{1,0:T(8,128)(2,1)}) custom-call(bf16[128,512]{1,0:T(8,128)(2,1)} %bitcast.10, bf16[128,512]{1,0:T(8,128)(2,1)} %start_codes.1, bf16[128,512]{1,0:T(8,128)(2,1)} %bitcast.11, bf16[128,512]{1,0:T(8,128)(2,1)} %loss_grads.1, bf16[512,512]{1,0:T(8,128)(2,1)} %bitcast.8, ...), custom_call_target="tpu_custom_call" | custom-call | tf_op jit(solution)/shard_map/pallas_call | solution.py:658
  89.4 0.0 copy-start
  89.4 1.6 %copy.14 = bf16[1,128,512]{2,1,0:T(8,128)(2,1)} copy(bf16[1,128,512]{2,1,0:T(8,128)(2,1)} %bitcast.15) | data formatting | bytes 262144
  91.0 0.0 copy-done
  91.0 0.7 copy.15
  (2 shorter events, 0.0 us)
Async XLA Ops:
  89.4 1.6 %copy-start = (bf16[128,512]{1,0:T(8,128)(2,1)S(1)}, bf16[128,512]{1,0:T(8,128)(2,1)}, u32[]{:S(2)}) copy-start(bf16[128,512]{1,0:T(8,128)(2,1)} %get-tuple-element.5) | copy-start | bytes 393220

commit v8 on v7

--- a/solution.py
+++ b/solution.py
@@ -292,30 +292,31 @@
 
     scale = HD ** (-0.5)
     scale_two = scale * LOG2_E
-    all_cols = 8 * TOK
     late = 4 * TOK
 
-    def own_mask(first_col):
-        shape = (TOK, all_cols - first_col)
-        key = lax.broadcasted_iota(jnp.int32, shape, 0) + c * TOK
-        col = lax.broadcasted_iota(jnp.int32, shape, 1) + first_col
+    def tile_cols(half_of):
+        return slice(half_of * late, (half_of + 1) * late)
+
+    def own_mask(half_of, keys):
+        shape = (keys, late)
+        key = lax.broadcasted_iota(jnp.int32, shape, 0)
+        col = lax.broadcasted_iota(jnp.int32, shape, 1)
         query = (col & (TOK - 1)) + ((col & (2 * TOK)) >> 1)
-        visible = key <= query
-        if first_col == 0:
-            visible = visible | (col >= late)
-        return visible
-
-    def forward_tile(kept, step, zz, xx, first_col, masked):
-        span = slice(first_col, all_cols)
-        block = rows((zz * 2 + xx) * TOK)
+        if half_of == 0:
+            return key + c * TOK <= query
+        return (key < TOK) | (key - TOK + c * TOK <= query)
+
+    def forward_tile(kept, step, zz, half_of, keys, masked):
+        span = tile_cols(half_of)
+        block = rows(zz * 2 * TOK, keys)
         scores = dot(kv[block, :HD], q_cols[:, span]) * scale_two
         if masked:
-            scores = jnp.where(own_mask(first_col), scores, 2 * MASK_FILL)
+            scores = jnp.where(own_mask(half_of, keys), scores, 2 * MASK_FILL)
         top_old = stats[0:1, span]
         top_new = jnp.maximum(top_old, jnp.max(scores, axis=0, keepdims=True))
         weights = jnp.exp2(scores - top_new)
-        kept_weights[kept, step, rows(xx * TOK), span] = weights
-        kept_tops[kept, step, xx : xx + 1, span] = top_new
+        kept_weights[kept, step, :keys, span] = weights
+        kept_tops[kept, step, half_of : half_of + 1, span] = top_new
         shrink = jnp.exp2(top_old - top_new)
         stats[1:2, span] = stats[1:2, span] * shrink + jnp.sum(weights, axis=0, keepdims=True)
         acc[:, span] = acc[:, span] * shrink + dot_first(kv[block, HD:], weights.astype(BF16))
@@ -344,12 +345,12 @@
 
         @pl.when(zz < z)
         def _():
-            forward_tile(kept, step, zz, 0, 0, False)
-            forward_tile(kept, step, zz, 1, late, False)
+            forward_tile(kept, step, zz, 1, 2 * TOK, False)
+            forward_tile(kept, step, zz, 0, TOK, False)
 
         @pl.when(zz > z)
         def _():
-            forward_tile(kept, step, zz, 0, late, False)
+            forward_tile(kept, step, zz, 1, TOK, False)
 
     def arrive_item(item):
         way, step = gathered(item)
@@ -367,15 +368,26 @@
     turn(q_rows, q_cols)
     kv_copy.wait_recv()
     relay_copy(0, 0, z, 1 - x).wait_recv()
-    forward_tile(0, 0, z, 0, 0, True)
-    forward_tile(0, 0, z, 1, late, True)
+    forward_tile(0, 0, z, 1, 2 * TOK, True)
+    forward_tile(0, 0, z, 0, TOK, True)
+
+    catches = (5 + ring // 4, 4 + ring // 2) if ring >= 16 else ()
+
+    def caught_up(item):
+        return sum(jnp.where(item >= catch, 1, 0) for catch in catches)
 
     def forward_step(item, carry):
         @pl.when(item < ring)
         def _():
             arrive_item(item)
 
-        forward_block(item - 4)
+        forward_block(item - 4 + caught_up(item - 1))
+
+        if catches:
+
+            @pl.when(caught_up(item) > caught_up(item - 1))
+            def _():
+                forward_block(item - 3 + caught_up(item - 1))
 
         @pl.when(item == 5 + ring // 4)
         def _():
@@ -405,7 +417,7 @@
 
         return carry
 
-    lax.fori_loop(5, ring + 4, forward_step, 0)
+    lax.fori_loop(5, ring + 4 - len(catches), forward_step, 0)
 
     acc_copy = copy_once(ACC_C, acc, acc_peer, other_core)
     stats_copy = copy_once(STATS_C, stats, stats_peer, other_core)
@@ -429,16 +441,21 @@
     )
     att_cols[...] = attended
 
-    def backward_tile(way, step, zz, xx, first_col):
-        span = slice(first_col, all_cols)
-        block = rows((zz * 2 + xx) * TOK)
-        out = rows(xx * TOK)
-        factor = jnp.exp2(kept_tops[1 - way, step, xx : xx + 1, span] - lse[:, span])
-        probs = kept_weights[1 - way, step, out, span] * factor
+    def backward_tile(way, step, zz, half_of, keys):
+        span = tile_cols(half_of)
+        block = rows(zz * 2 * TOK, keys)
+        factor = jnp.exp2(kept_tops[1 - way, step, half_of : half_of + 1, span] - lse[:, span])
+        probs = kept_weights[1 - way, step, :keys, span] * factor
         grad_prob = dot(kv[block, HD:], do_cols[:, span])
         grad_score = (probs * (grad_prob - delta[:, span]) * scale).astype(BF16)
-        part[way, step, out, HD:] = dot(probs.astype(BF16), do_rows[span, :])
-        part[way, step, out, :HD] = dot(grad_score, q_rows[span, :])
+        value_grad = dot(probs.astype(BF16), do_rows[span, :])
+        key_grad = dot(grad_score, q_rows[span, :])
+        if half_of == 1:
+            part[way, step, :keys, HD:] = value_grad
+            part[way, step, :keys, :HD] = key_grad
+        else:
+            part[way, step, :keys, HD:] += value_grad
+            part[way, step, :keys, :HD] += key_grad
         dq_cols[:, span] += dot_first(kv[block, :HD], grad_score)
 
     def leaving(item):
@@ -463,12 +480,12 @@
 
         @pl.when(zz <= z)
         def _():
-            backward_tile(way, step, zz, 0, 0)
-            backward_tile(way, step, zz, 1, late)
+            backward_tile(way, step, zz, 1, 2 * TOK)
+            backward_tile(way, step, zz, 0, TOK)
 
         @pl.when(zz > z)
         def _():
-            backward_tile(way, step, zz, 0, late)
+            backward_tile(way, step, zz, 1, TOK)
             part[way, step, TOK:, :] = jnp.zeros((TOK, 2 * HD), F32)
 
         cross_out[way, step] = own_part(way, step, 3).astype(BF16)
@@ -626,6 +643,15 @@
 
     relay_copy(0, 0, z, x).wait_send()
     lax.fori_loop(ring - 3, ring, settle_reduce, 0)
+
+
+def hand_over(codes, grads, out_codes, in_grads, sems):
+    pairs = ((codes, out_codes), (grads, in_grads))
+    copies = [pltpu.make_async_copy(src, dst, sems.at[i]) for i, (src, dst) in enumerate(pairs)]
+    for one in copies:
+        one.start()
+    for one in copies:
+        one.wait()
 
 
 def rope_tables(first_pos):
@@ -733,6 +759,14 @@
         cosines,
         sines,
     )
+    results = pl.pallas_call(
+        hand_over,
+        out_shape=(jax.ShapeDtypeStruct(one_block, BF16),) * 2,
+        in_specs=[pl.BlockSpec(memory_space=pl.ANY)] * 2,
+        out_specs=(pl.BlockSpec(memory_space=pl.ANY),) * 2,
+        scratch_shapes=[dma((2,))],
+        compiler_params=pltpu.CompilerParams(vmem_limit_bytes=60 * 1024 * 1024),
+    )(*results)
     return (results[0][None], results[1][None])
 
 

time: 92.4 us -> 100 us (1.082)
  Pallas kernels: 87.9 us -> 97.6 us
  local copies, waits for them, and re-layouts: 2.26 us -> 0 us
    pallas_call x0 -> x1, Pallas kernels: none -> 9.06 us  [local(): pl.pallas_call(hand_over, out_shape=(jax.ShapeDtypeStruct(one_block, BF16...]
    unnamed x4 -> x0, local copies, waits for them, and re-layouts: 2.26 us -> none
where the time goes in v8:
time: 100 us; the launch traced here: 99.1 us
  Pallas kernels  97.6 us (98%)
    pallas_call x1, Pallas kernels, local(): pl.pallas_call(functools.partial(kernel, ring, sections), out_shape=(jax....  88.6 us
    pallas_call x1, Pallas kernels, local(): pl.pallas_call(hand_over, out_shape=(jax.ShapeDtypeStruct(one_block, BF16...  9.06 us

profile of v8, /device:TPU:6, one launch (start us, length us, event | category | flops | bytes accessed | tf_op | source)
XLA Modules:
  0.0 99.1 jit_solution(6795451503184403056)
XLA Ops:
  0.6 0.1 pad_maximum_fusion
  0.7 0.8 fusion
  1.5 88.6 %shard_map.113 = (bf16[128,512]{1,0:T(8,128)(2,1)}, bf16[128,512]{1,0:T(8,128)(2,1)}) custom-call(bf16[128,512]{1,0:T(8,128)(2,1)} %bitcast.10, bf16[128,512]{1,0:T(8,128)(2,1)} %start_codes.1, bf16[128,512]{1,0:T(8,128)(2,1)} %bitcast.11, bf16[128,512]{1,0:T(8,128)(2,1)} %loss_grads.1, bf16[512,512]{1,0:T(8,128)(2,1)} %bitcast.8, ...), custom_call_target="tpu_custom_call" | custom-call | tf_op jit(solution)/shard_map/pallas_call | solution.py:684
  90.1 9.1 %shard_map.114 = (bf16[128,512]{1,0:T(8,128)(2,1)}, bf16[128,512]{1,0:T(8,128)(2,1)}) custom-call(bf16[128,512]{1,0:T(8,128)(2,1)} %get-tuple-element.6.codes, bf16[128,512]{1,0:T(8,128)(2,1)} %get-tuple-element.7.grads), custom_call_target="tpu_custom_call" | custom-call | tf_op jit(solution)/shard_map/pallas_call | solution.py:762
  (2 shorter events, 0.0 us)

commit v9 on v8

--- a/solution.py
+++ b/solution.py
@@ -62,6 +62,8 @@
     w_key,
     w_value,
     w_out,
+    codes_out,
+    grads_out,
     codes_edge,
     grads_edge,
     codes_buf,
@@ -151,10 +153,12 @@
         pltpu.make_async_copy(src, dst, load_sems.at[number])
         for number, (src, dst) in enumerate(
             (
+                (sent_codes, codes_out),
                 (start_codes, codes_edge),
                 (w_key_hbm, w_key),
                 (w_value_hbm, w_value),
                 (w_query_hbm, w_query),
+                (sent_grads, grads_out),
                 (loss_grads, grads_edge),
                 (w_out_hbm, w_out),
             )
@@ -169,8 +173,9 @@
         pl.semaphore_signal(barrier, inc=1, device_id=partner, device_id_type=MESH)
     pl.semaphore_wait(barrier, 8)
 
-    codes_copy = copy_once(CODES, sent_codes, codes_buf, next_section)
-    grads_copy = copy_once(GRADS, sent_grads, grads_buf, last_section)
+    codes_copy = copy_once(CODES, codes_out, codes_buf, next_section)
+    grads_copy = copy_once(GRADS, grads_out, grads_buf, last_section)
+    loads[0].wait()
     codes_copy.start()
 
     stats[...] = jnp.where(
@@ -246,7 +251,7 @@
             span = slice(block * TOK, (block + 1) * TOK)
             dst[:, span] = src[span, :].T
 
-    for load in loads[:3]:
+    for load in loads[1:4]:
         load.wait()
     codes_copy.wait_recv()
 
@@ -278,7 +283,7 @@
     kv_copy.start()
     relay_copy(0, 0, z, x).start()
 
-    loads[3].wait()
+    loads[4].wait()
     q_lin[...] = dot(normed, w_query[...])
     for head in range(4):
         q_own[head * TOK : (head + 1) * TOK, :] = head_norm(
@@ -288,6 +293,7 @@
     q_copies[1].start()
     q_rows[own_rows, :] = q_own[own_heads, :]
 
+    loads[5].wait()
     grads_copy.start()
 
     scale = HD ** (-0.5)
@@ -391,7 +397,7 @@
 
         @pl.when(item == 5 + ring // 4)
         def _():
-            for load in loads[4:]:
+            for load in loads[6:]:
                 load.wait()
             grads_copy.wait_recv()
 
@@ -643,15 +649,6 @@
 
     relay_copy(0, 0, z, x).wait_send()
     lax.fori_loop(ring - 3, ring, settle_reduce, 0)
-
-
-def hand_over(codes, grads, out_codes, in_grads, sems):
-    pairs = ((codes, out_codes), (grads, in_grads))
-    copies = [pltpu.make_async_copy(src, dst, sems.at[i]) for i, (src, dst) in enumerate(pairs)]
-    for one in copies:
-        one.start()
-    for one in copies:
-        one.wait()
 
 
 def rope_tables(first_pos):
@@ -691,6 +688,8 @@
             vmem(w_key.shape[1:], BF16),
             vmem(w_value.shape[1:], BF16),
             vmem(w_out.shape[1:], BF16),
+            vmem(one_block, BF16),
+            vmem(one_block, BF16),
             vmem(one_block, BF16),
             vmem(one_block, BF16),
             vmem(one_block, BF16),
@@ -740,7 +739,7 @@
             dma((2, steps)),
             dma((2, steps)),
             dma((2, steps)),
-            dma((6,)),
+            dma((8,)),
         ],
         compiler_params=pltpu.CompilerParams(
             collective_id=0, has_side_effects=True, vmem_limit_bytes=60 * 1024 * 1024
@@ -759,14 +758,6 @@
         cosines,
         sines,
     )
-    results = pl.pallas_call(
-        hand_over,
-        out_shape=(jax.ShapeDtypeStruct(one_block, BF16),) * 2,
-        in_specs=[pl.BlockSpec(memory_space=pl.ANY)] * 2,
-        out_specs=(pl.BlockSpec(memory_space=pl.ANY),) * 2,
-        scratch_shapes=[dma((2,))],
-        compiler_params=pltpu.CompilerParams(vmem_limit_bytes=60 * 1024 * 1024),
-    )(*results)
     return (results[0][None], results[1][None])
 
 

time: 100 us -> 92.8 us (0.928)
  Pallas kernels: 97.6 us -> 88.3 us
  local copies, waits for them, and re-layouts: 0 us -> 2.26 us
    pallas_call x1 -> x0, Pallas kernels: 9.06 us -> none  [local(): pl.pallas_call(hand_over, out_shape=(jax.ShapeDtypeStruct(one_block, BF16...]
    unnamed x0 -> x4, local copies, waits for them, and re-layouts: none -> 2.26 us
where the time goes in v9:
time: 92.8 us; the launch traced here: 92 us
  Pallas kernels  88.3 us (95%)
  local copies, waits for them, and re-layouts  2.26 us (2%)
    pallas_call x1, Pallas kernels, local(): pl.pallas_call(functools.partial(kernel, ring, sections), out_shape=(jax....  88.3 us
    unnamed x4, local copies, waits for them, and re-layouts  2.26 us

profile of v9, /device:TPU:6, one launch (start us, length us, event | category | flops | bytes accessed | tf_op | source)
XLA Modules:
  0.0 92.0 jit_solution(2116934594854215165)
XLA Ops:
  0.6 0.1 pad_maximum_fusion
  0.7 0.8 fusion
  1.5 88.3 %shard_map.113 = (bf16[128,512]{1,0:T(8,128)(2,1)}, bf16[128,512]{1,0:T(8,128)(2,1)}) custom-call(bf16[128,512]{1,0:T(8,128)(2,1)} %bitcast.10, bf16[128,512]{1,0:T(8,128)(2,1)} %start_codes.1, bf16[128,512]{1,0:T(8,128)(2,1)} %bitcast.11, bf16[128,512]{1,0:T(8,128)(2,1)} %loss_grads.1, bf16[512,512]{1,0:T(8,128)(2,1)} %bitcast.8, ...), custom_call_target="tpu_custom_call" | custom-call | tf_op jit(solution)/shard_map/pallas_call | solution.py:681
  89.8 0.0 copy-start
  89.8 1.6 %copy.14 = bf16[1,128,512]{2,1,0:T(8,128)(2,1)} copy(bf16[1,128,512]{2,1,0:T(8,128)(2,1)} %bitcast.15) | data formatting | bytes 262144
  91.4 0.0 copy-done
  91.4 0.7 copy.15
  (2 shorter events, 0.0 us)
Async XLA Ops:
  89.8 1.6 %copy-start = (bf16[128,512]{1,0:T(8,128)(2,1)S(1)}, bf16[128,512]{1,0:T(8,128)(2,1)}, u32[]{:S(2)}) copy-start(bf16[128,512]{1,0:T(8,128)(2,1)} %get-tuple-element.5) | copy-start | bytes 393220

commit v10 on v9

--- a/solution.py
+++ b/solution.py
@@ -125,11 +125,11 @@
     def device(xx, zz, cc):
         return (sec, (xx * ring + zz) * 2 + cc)
 
-    def along(way):
-        return device(x, lax.rem(z + 1 + way * (ring - 2), ring), c)
-
-    def diagonal(way):
-        return device(1 - x, lax.rem(z + 1 + way * (ring - 2), ring), c)
+    def along(way, hops=1):
+        return device(x, lax.rem(z + hops + way * (ring - 2 * hops), ring), c)
+
+    def diagonal(way, hops=1):
+        return device(1 - x, lax.rem(z + hops + way * (ring - 2 * hops), ring), c)
 
     other_core = device(x, z, 1 - c)
     across = device(1 - x, z, c)
@@ -168,10 +168,11 @@
         load.start()
 
     barrier = pltpu.get_barrier_semaphore()
-    partners = (along(0), along(1), diagonal(0), diagonal(1), other_core, across)
-    for partner in (*partners, next_section, last_section):
+    near = [(way, hops) for way in range(2) for hops in (1, 2)]
+    partners = [along(*one) for one in near] + [diagonal(*one) for one in near]
+    for partner in (*partners, other_core, across, next_section, last_section):
         pl.semaphore_signal(barrier, inc=1, device_id=partner, device_id_type=MESH)
-    pl.semaphore_wait(barrier, 8)
+    pl.semaphore_wait(barrier, 12)
 
     codes_copy = copy_once(CODES, codes_out, codes_buf, next_section)
     grads_copy = copy_once(GRADS, grads_out, grads_buf, last_section)
@@ -184,7 +185,8 @@
     acc[...] = jnp.zeros(acc.shape, F32)
     dq_cols[...] = jnp.zeros(dq_cols.shape, F32)
     for way, farthest in ((0, half), (1, half - 1)):
-        ring_in[way, farthest] = jnp.zeros(ring_in.shape[2:], BF16)
+        if farthest > 1:
+            ring_in[way, farthest] = jnp.zeros(ring_in.shape[2:], BF16)
 
     lane = lax.broadcasted_iota(jnp.int32, (TOK, HD), 1)
     first_half = lane < HD // 2
@@ -222,10 +224,10 @@
     def place(way, step):
         return lax.rem(z + way * step + (1 - way) * (ring - step), ring)
 
-    def gather_copy(way, step, piece, zz):
+    def gather_copy(way, step, piece, zz, hops=1):
         ref = piece_of(piece, zz)
         sems = (gather_send.at[way, step, piece], gather_recv.at[way, step, piece])
-        return copy(ref, ref, *sems, along(way))
+        return copy(ref, ref, *sems, along(way, hops))
 
     def relay_copy(way, step, zz, xx):
         ref = piece_of(3, zz, xx)
@@ -273,12 +275,12 @@
     kv[own, HD:] = dot(normed, w_value[...]).astype(BF16)
 
     first_piece = piece_of(0, z, x)
-    for piece in (1, 0):
-        for way in range(2):
-            gather_copy(way, 1, piece, z).start()
-    for way in range(2):
-        sems = (gather_send.at[way, 1, 2], gather_recv.at[way, 1, 2])
-        copy(first_piece, first_piece, *sems, diagonal(way)).start()
+    reached = [(way, hops) for hops in (1, 2) for way in range(2) if hops <= half - way]
+    for way, hops in reached:
+        for piece in (1, 0):
+            gather_copy(way, hops, piece, z, hops).start()
+        sems = (gather_send.at[way, hops, 2], gather_recv.at[way, hops, 2])
+        copy(first_piece, first_piece, *sems, diagonal(way, hops)).start()
     kv_copy = copy_once(KV_X, first_piece, first_piece, across)
     kv_copy.start()
     relay_copy(0, 0, z, x).start()
@@ -360,7 +362,7 @@
 
     def arrive_item(item):
         way, step = gathered(item)
-        arrive(way, step, step < half - way)
+        arrive(way, step, (step > 1) & (step < half - way))
 
     arrive_item(1)
     arrive_item(2)
@@ -497,32 +499,40 @@
         cross_out[way, step] = own_part(way, step, 3).astype(BF16)
         cross_copy(way, step).start()
 
-    def reduce_copy(way, step, piece, target=None):
+    def reduce_copy(way, step, piece, near=None):
         span = slice(piece * PIECE, (piece + 1) * PIECE)
+        if near is None:
+            slot, target = step - 1, along(way)
+        else:
+            slot, target = 2 - near, (diagonal if piece == 2 else along)(way, near)
         return copy(
             ring_out.at[way, step, span],
-            ring_in.at[way, step - 1, span],
+            ring_in.at[way, slot, span],
             reduce_send.at[way, step, piece],
-            reduce_recv.at[way, step - 1, piece],
-            along(way) if target is None else target,
+            reduce_recv.at[way, slot, piece],
+            target,
         )
 
-    def reduce_step(item, last=False):
+    def reduce_step(item, static=False):
         way, step = leaving(item)
+        near = None
+        if static and item >= ring - 5:
+            near = 2 if item < ring - 3 else 1
         for piece in (0, 2, 1):
-
-            @pl.when(step < half - way)
-            def _():
-                reduce_copy(way, step + 1, piece).wait_recv()
-
             span = slice(piece * PIECE, (piece + 1) * PIECE)
-            summed = own_part(way, step, piece) + ring_in[way, step, span].astype(F32)
+            summed = own_part(way, step, piece)
+            if near != 1:
+
+                @pl.when(step < half - way)
+                def _():
+                    reduce_copy(way, step + 1, piece).wait_recv()
+
+                summed = summed + ring_in[way, step, span].astype(F32)
             if piece == 1:
                 cross_copy(way, step).wait_recv()
                 summed = summed + cross_in[way, step].astype(F32)
             ring_out[way, step, span] = summed.astype(BF16)
-            target = diagonal(way) if last and piece == 2 else None
-            reduce_copy(way, step, piece, target).start()
+            reduce_copy(way, step, piece, near).start()
 
     def backward_step(count, carry):
         block = 2 + 3 * count
@@ -543,7 +553,7 @@
     backward_block(1)
     lax.fori_loop(0, rounds, backward_step, 0)
     backward_block(ring - 2)
-    reduce_step(reduced)
+    reduce_step(reduced, True)
     backward_block(ring - 1)
 
     kv_send[...] = own_part(1, 0, 2).astype(BF16)
@@ -564,7 +574,7 @@
     ]
     for number in range(2):
         dq_core_copies[number].start()
-    reduce_step(reduced + 1, reduced + 1 >= ring - 3)
+    reduce_step(reduced + 1, True)
 
     def settle_gather(item, carry):
         way, step = gathered(item)
@@ -599,8 +609,8 @@
     att_copy.start()
     att_own[own_heads, :] = att_rows[own_heads, :]
 
-    lax.fori_loop(reduced + 2, ring - 3, reduce_only, 0)
-    for item in range(max(reduced + 2, ring - 3), ring - 1):
+    lax.fori_loop(reduced + 2, ring - 5, reduce_only, 0)
+    for item in range(max(reduced + 2, ring - 5), ring - 1):
         reduce_step(item, True)
     lax.fori_loop(0, ring - 3, settle_reduce, 0)
 
@@ -619,10 +629,12 @@
         normed_grad = normed_grad + dot_last(lin_grad, w_query[:, span])
 
     def ringed(piece):
-        for way in range(2):
-            reduce_copy(way, 1, piece).wait_recv()
         span = slice(piece * PIECE, (piece + 1) * PIECE)
-        return ring_in[0, 0, span].astype(F32) + ring_in[1, 0, span].astype(F32)
+        summed = 0.0
+        for way, hops in reached:
+            reduce_copy(way, hops, piece, hops).wait_recv()
+            summed = summed + ring_in[way, 2 - hops, span].astype(F32)
+        return summed
 
     cross_copy(1, 0).wait_recv()
     dkv_copy.wait_recv()

time: 92.8 us -> 94 us (1.013)
  no operation moved by 1% of the time
where the time goes in v10:
time: 94 us; the launch traced here: 92.4 us
  Pallas kernels  88.6 us (94%)
  local copies, waits for them, and re-layouts  2.26 us (2%)
    pallas_call x1, Pallas kernels, local(): pl.pallas_call(functools.partial(kernel, ring, sections), out_shape=(jax....  88.6 us
    unnamed x4, local copies, waits for them, and re-layouts  2.26 us

profile of v10, /device:TPU:6, one launch (start us, length us, event | category | flops | bytes accessed | tf_op | source)
XLA Modules:
  0.0 92.4 jit_solution(11687352808665112641)
XLA Ops:
  0.6 0.1 pad_maximum_fusion
  0.7 0.8 fusion
  1.5 88.6 %shard_map.113 = (bf16[128,512]{1,0:T(8,128)(2,1)}, bf16[128,512]{1,0:T(8,128)(2,1)}) custom-call(bf16[128,512]{1,0:T(8,128)(2,1)} %bitcast.10, bf16[128,512]{1,0:T(8,128)(2,1)} %start_codes.1, bf16[128,512]{1,0:T(8,128)(2,1)} %bitcast.11, bf16[128,512]{1,0:T(8,128)(2,1)} %loss_grads.1, bf16[512,512]{1,0:T(8,128)(2,1)} %bitcast.8, ...), custom_call_target="tpu_custom_call" | custom-call | tf_op jit(solution)/shard_map/pallas_call | solution.py:693
  90.1 0.0 copy-start
  90.1 1.6 %copy.14 = bf16[1,128,512]{2,1,0:T(8,128)(2,1)} copy(bf16[1,128,512]{2,1,0:T(8,128)(2,1)} %bitcast.15) | data formatting | bytes 262144
  91.7 0.0 copy-done
  91.7 0.7 copy.15
  (2 shorter events, 0.0 us)
Async XLA Ops:
  90.1 1.6 %copy-start = (bf16[128,512]{1,0:T(8,128)(2,1)S(1)}, bf16[128,512]{1,0:T(8,128)(2,1)}, u32[]{:S(2)}) copy-start(bf16[128,512]{1,0:T(8,128)(2,1)} %get-tuple-element.5) | copy-start | bytes 393220

commit v11 on v9

--- a/solution.py
+++ b/solution.py
@@ -300,33 +300,44 @@
     scale_two = scale * LOG2_E
     late = 4 * TOK
 
-    def tile_cols(half_of):
-        return slice(half_of * late, (half_of + 1) * late)
-
-    def own_mask(half_of, keys):
-        shape = (keys, late)
+    wide_chain = 2 * TOK
+    late_chains = (late, late + wide_chain)
+    early_chains = (0, wide_chain)
+    seen_chains = [(2 * TOK, col) for col in late_chains] + [(TOK, col) for col in early_chains]
+    unseen_chains = [(TOK, col) for col in late_chains]
+
+    def own_mask(keys, first_col):
+        shape = (keys, wide_chain)
         key = lax.broadcasted_iota(jnp.int32, shape, 0)
         col = lax.broadcasted_iota(jnp.int32, shape, 1)
-        query = (col & (TOK - 1)) + ((col & (2 * TOK)) >> 1)
-        if half_of == 0:
+        query = (col & (TOK - 1)) + first_col % late // 2
+        if first_col < late:
             return key + c * TOK <= query
         return (key < TOK) | (key - TOK + c * TOK <= query)
 
-    def forward_tile(kept, step, zz, half_of, keys, masked):
-        span = tile_cols(half_of)
-        block = rows(zz * 2 * TOK, keys)
-        scores = dot(kv[block, :HD], q_cols[:, span]) * scale_two
-        if masked:
-            scores = jnp.where(own_mask(half_of, keys), scores, 2 * MASK_FILL)
-        top_old = stats[0:1, span]
-        top_new = jnp.maximum(top_old, jnp.max(scores, axis=0, keepdims=True))
-        weights = jnp.exp2(scores - top_new)
-        kept_weights[kept, step, :keys, span] = weights
-        kept_tops[kept, step, half_of : half_of + 1, span] = top_new
-        shrink = jnp.exp2(top_old - top_new)
-        stats[1:2, span] = stats[1:2, span] * shrink + jnp.sum(weights, axis=0, keepdims=True)
-        acc[:, span] = acc[:, span] * shrink + dot_first(kv[block, HD:], weights.astype(BF16))
-        stats[0:1, span] = top_new
+    def forward_chains(kept, step, zz, chains, masked):
+        def raw_scores(keys, first_col):
+            block = rows(zz * 2 * TOK, keys)
+            return dot(kv[block, :HD], q_cols[:, first_col : first_col + wide_chain])
+
+        following = raw_scores(*chains[0])
+        for number, (keys, first_col) in enumerate(chains):
+            scores = following * scale_two
+            if number + 1 < len(chains):
+                following = raw_scores(*chains[number + 1])
+            span = slice(first_col, first_col + wide_chain)
+            block = rows(zz * 2 * TOK, keys)
+            if masked:
+                scores = jnp.where(own_mask(keys, first_col), scores, 2 * MASK_FILL)
+            top_old = stats[0:1, span]
+            top_new = jnp.maximum(top_old, jnp.max(scores, axis=0, keepdims=True))
+            weights = jnp.exp2(scores - top_new)
+            kept_weights[kept, step, :keys, span] = weights
+            kept_tops[kept, step, 0:1, span] = top_new
+            shrink = jnp.exp2(top_old - top_new)
+            stats[1:2, span] = stats[1:2, span] * shrink + jnp.sum(weights, axis=0, keepdims=True)
+            acc[:, span] = acc[:, span] * shrink + dot_first(kv[block, HD:], weights.astype(BF16))
+            stats[0:1, span] = top_new
 
     def arrive(way, step, forward):
         zz = place(way, step)
@@ -351,12 +362,11 @@
 
         @pl.when(zz < z)
         def _():
-            forward_tile(kept, step, zz, 1, 2 * TOK, False)
-            forward_tile(kept, step, zz, 0, TOK, False)
+            forward_chains(kept, step, zz, seen_chains, False)
 
         @pl.when(zz > z)
         def _():
-            forward_tile(kept, step, zz, 1, TOK, False)
+            forward_chains(kept, step, zz, unseen_chains, False)
 
     def arrive_item(item):
         way, step = gathered(item)
@@ -374,8 +384,7 @@
     turn(q_rows, q_cols)
     kv_copy.wait_recv()
     relay_copy(0, 0, z, 1 - x).wait_recv()
-    forward_tile(0, 0, z, 1, 2 * TOK, True)
-    forward_tile(0, 0, z, 0, TOK, True)
+    forward_chains(0, 0, z, seen_chains, True)
 
     catches = (5 + ring // 4, 4 + ring // 2) if ring >= 16 else ()
 
@@ -447,22 +456,38 @@
     )
     att_cols[...] = attended
 
-    def backward_tile(way, step, zz, half_of, keys):
-        span = tile_cols(half_of)
-        block = rows(zz * 2 * TOK, keys)
-        factor = jnp.exp2(kept_tops[1 - way, step, half_of : half_of + 1, span] - lse[:, span])
-        probs = kept_weights[1 - way, step, :keys, span] * factor
-        grad_prob = dot(kv[block, HD:], do_cols[:, span])
-        grad_score = (probs * (grad_prob - delta[:, span]) * scale).astype(BF16)
-        value_grad = dot(probs.astype(BF16), do_rows[span, :])
-        key_grad = dot(grad_score, q_rows[span, :])
-        if half_of == 1:
-            part[way, step, :keys, HD:] = value_grad
-            part[way, step, :keys, :HD] = key_grad
-        else:
-            part[way, step, :keys, HD:] += value_grad
-            part[way, step, :keys, :HD] += key_grad
-        dq_cols[:, span] += dot_first(kv[block, :HD], grad_score)
+    def backward_chains(way, step, zz, chains):
+        def raw_grads(keys, first_col):
+            block = rows(zz * 2 * TOK, keys)
+            return dot(kv[block, HD:], do_cols[:, first_col : first_col + wide_chain])
+
+        sums = {}
+
+        def add(keys, name, term):
+            sums[keys, name] = sums[keys, name] + term if (keys, name) in sums else term
+
+        following = raw_grads(*chains[0])
+        for number, (keys, first_col) in enumerate(chains):
+            grad_prob = following
+            if number + 1 < len(chains):
+                following = raw_grads(*chains[number + 1])
+            span = slice(first_col, first_col + wide_chain)
+            block = rows(zz * 2 * TOK, keys)
+            factor = jnp.exp2(kept_tops[1 - way, step, 0:1, span] - lse[:, span])
+            probs = kept_weights[1 - way, step, :keys, span] * factor
+            grad_score = (probs * (grad_prob - delta[:, span]) * scale).astype(BF16)
+            add(keys, 0, dot(grad_score, q_rows[span, :]))
+            add(keys, 1, dot(probs.astype(BF16), do_rows[span, :]))
+            dq_cols[:, span] += dot_first(kv[block, :HD], grad_score)
+        for name in range(2):
+            cols = slice(name * HD, (name + 1) * HD)
+            if (2 * TOK, name) in sums:
+                both = sums[2 * TOK, name]
+                part[way, step, :TOK, cols] = both[:TOK] + sums[TOK, name]
+                part[way, step, TOK:, cols] = both[TOK:]
+            else:
+                part[way, step, :TOK, cols] = sums[TOK, name]
+                part[way, step, TOK:, cols] = jnp.zeros((TOK, HD), F32)
 
     def leaving(item):
         return lax.rem(item, 2), half - lax.div(item + 1, 2)
@@ -486,13 +511,11 @@
 
         @pl.when(zz <= z)
         def _():
-            backward_tile(way, step, zz, 1, 2 * TOK)
-            backward_tile(way, step, zz, 0, TOK)
+            backward_chains(way, step, zz, seen_chains)
 
         @pl.when(zz > z)
         def _():
-            backward_tile(way, step, zz, 1, TOK)
-            part[way, step, TOK:, :] = jnp.zeros((TOK, 2 * HD), F32)
+            backward_chains(way, step, zz, unseen_chains)
 
         cross_out[way, step] = own_part(way, step, 3).astype(BF16)
         cross_copy(way, step).start()

time: 92.8 us -> 92.6 us (level)
  no operation moved by 1% of the time
where the time goes in v11:
time: 92.6 us; the launch traced here: 91.4 us
  Pallas kernels  87.6 us (95%)
  local copies, waits for them, and re-layouts  2.26 us (2%)
    pallas_call x1, Pallas kernels, local(): pl.pallas_call(functools.partial(kernel, ring, sections), out_shape=(jax....  87.6 us
    unnamed x4, local copies, waits for them, and re-layouts  2.26 us

profile of v11, /device:TPU:6, one launch (start us, length us, event | category | flops | bytes accessed | tf_op | source)
XLA Modules:
  0.0 91.4 jit_solution(13052335438691170097)
XLA Ops:
  0.6 0.1 pad_maximum_fusion
  0.7 0.8 fusion
  1.5 87.6 %shard_map.113 = (bf16[128,512]{1,0:T(8,128)(2,1)}, bf16[128,512]{1,0:T(8,128)(2,1)}) custom-call(bf16[128,512]{1,0:T(8,128)(2,1)} %bitcast.10, bf16[128,512]{1,0:T(8,128)(2,1)} %start_codes.1, bf16[128,512]{1,0:T(8,128)(2,1)} %bitcast.11, bf16[128,512]{1,0:T(8,128)(2,1)} %loss_grads.1, bf16[512,512]{1,0:T(8,128)(2,1)} %bitcast.8, ...), custom_call_target="tpu_custom_call" | custom-call | tf_op jit(solution)/shard_map/pallas_call | solution.py:704
  89.1 0.0 copy-start
  89.1 1.6 %copy.14 = bf16[1,128,512]{2,1,0:T(8,128)(2,1)} copy(bf16[1,128,512]{2,1,0:T(8,128)(2,1)} %bitcast.15) | data formatting | bytes 262144
  90.7 0.0 copy-done
  90.7 0.7 copy.15
  (2 shorter events, 0.0 us)
Async XLA Ops:
  89.1 1.6 %copy-start = (bf16[128,512]{1,0:T(8,128)(2,1)S(1)}, bf16[128,512]{1,0:T(8,128)(2,1)}, u32[]{:S(2)}) copy-start(bf16[128,512]{1,0:T(8,128)(2,1)} %get-tuple-element.5) | copy-start | bytes 393220

commit v12 on v11

--- a/solution.py
+++ b/solution.py
@@ -215,9 +215,9 @@
 
     def piece_of(piece, zz, xx=None):
         if xx is None:
-            xx = x if piece < 2 else 1 - x
+            xx = x if piece == 0 else 1 - x
         start = (zz * 2 + xx) * TOK + piece % 2 * PIECE
-        return kv.at[pl.ds(pl.multiple_of(start, PIECE), PIECE)]
+        return kv.at[pl.ds(pl.multiple_of(start, PIECE), TOK if piece == 0 else PIECE)]
 
     def place(way, step):
         return lax.rem(z + way * step + (1 - way) * (ring - step), ring)
@@ -272,10 +272,9 @@
     kv[own, :HD] = head_norm(key_lin, k_gain[...])
     kv[own, HD:] = dot(normed, w_value[...]).astype(BF16)
 
-    first_piece = piece_of(0, z, x)
-    for piece in (1, 0):
-        for way in range(2):
-            gather_copy(way, 1, piece, z).start()
+    first_piece = piece_of(2, z, x)
+    for way in range(2):
+        gather_copy(way, 1, 0, z).start()
     for way in range(2):
         sems = (gather_send.at[way, 1, 2], gather_recv.at[way, 1, 2])
         copy(first_piece, first_piece, *sems, diagonal(way)).start()
@@ -341,14 +340,14 @@
 
     def arrive(way, step, forward):
         zz = place(way, step)
-        for piece in (1, 0, 2):
+        for piece in (0, 2):
             gather_copy(way, step, piece, zz).wait_recv()
 
             @pl.when(forward)
             def _():
                 gather_copy(way, step + 1, piece, zz).start()
 
-            if piece == 1:
+            if piece == 0:
                 relay_copy(way, step, zz, x).start()
 
     def gathered(item):
@@ -521,7 +520,7 @@
         cross_copy(way, step).start()
 
     def reduce_copy(way, step, piece, target=None):
-        span = slice(piece * PIECE, (piece + 1) * PIECE)
+        span = slice(0, TOK) if piece == 0 else slice(TOK, TOK + PIECE)
         return copy(
             ring_out.at[way, step, span],
             ring_in.at[way, step - 1, span],
@@ -532,18 +531,19 @@
 
     def reduce_step(item, last=False):
         way, step = leaving(item)
-        for piece in (0, 2, 1):
+        for piece in (2, 0):
 
             @pl.when(step < half - way)
             def _():
                 reduce_copy(way, step + 1, piece).wait_recv()
 
-            span = slice(piece * PIECE, (piece + 1) * PIECE)
-            summed = own_part(way, step, piece) + ring_in[way, step, span].astype(F32)
-            if piece == 1:
-                cross_copy(way, step).wait_recv()
-                summed = summed + cross_in[way, step].astype(F32)
-            ring_out[way, step, span] = summed.astype(BF16)
+            for part_piece in (2,) if piece == 2 else (0, 1):
+                span = slice(part_piece * PIECE, (part_piece + 1) * PIECE)
+                summed = own_part(way, step, part_piece) + ring_in[way, step, span].astype(F32)
+                if part_piece == 1:
+                    cross_copy(way, step).wait_recv()
+                    summed = summed + cross_in[way, step].astype(F32)
+                ring_out[way, step, span] = summed.astype(BF16)
             target = diagonal(way) if last and piece == 2 else None
             reduce_copy(way, step, piece, target).start()
 
@@ -592,7 +592,7 @@
     def settle_gather(item, carry):
         way, step = gathered(item)
         relay_copy(way, step, z, x).wait_send()
-        for piece in range(3):
+        for piece in (0, 2):
             gather_copy(way, step, piece, z).wait_send()
         return carry
 
@@ -602,7 +602,7 @@
 
         @pl.when(step > 0)
         def _():
-            for piece in range(3):
+            for piece in (0, 2):
                 reduce_copy(way, step, piece).wait_send()
 
         return carry
@@ -642,10 +642,12 @@
         normed_grad = normed_grad + dot_last(lin_grad, w_query[:, span])
 
     def ringed(piece):
+        span = slice(piece * PIECE, (piece + 1) * PIECE)
+        return ring_in[0, 0, span].astype(F32) + ring_in[1, 0, span].astype(F32)
+
+    for piece in (0, 2):
         for way in range(2):
             reduce_copy(way, 1, piece).wait_recv()
-        span = slice(piece * PIECE, (piece + 1) * PIECE)
-        return ring_in[0, 0, span].astype(F32) + ring_in[1, 0, span].astype(F32)
 
     cross_copy(1, 0).wait_recv()
     dkv_copy.wait_recv()

time: 92.6 us -> 95 us (1.026)
  Pallas kernels: 87.6 us -> 90.5 us
    pallas_call x1, Pallas kernels: 87.6 us -> 90.5 us  [local(): pl.pallas_call(functools.partial(kernel, ring, sections), out_shape=(jax....]
where the time goes in v12:
time: 95 us; the launch traced here: 94.2 us
  Pallas kernels  90.5 us (95%)
  local copies, waits for them, and re-layouts  2.26 us (2%)
    pallas_call x1, Pallas kernels, local(): pl.pallas_call(functools.partial(kernel, ring, sections), out_shape=(jax....  90.5 us
    unnamed x4, local copies, waits for them, and re-layouts  2.26 us

profile of v12, /device:TPU:6, one launch (start us, length us, event | category | flops | bytes accessed | tf_op | source)
XLA Modules:
  0.0 94.2 jit_solution(10056202190938815957)
XLA Ops:
  0.6 0.1 pad_maximum_fusion
  0.7 0.8 fusion
  1.5 90.5 %shard_map.113 = (bf16[128,512]{1,0:T(8,128)(2,1)}, bf16[128,512]{1,0:T(8,128)(2,1)}) custom-call(bf16[128,512]{1,0:T(8,128)(2,1)} %bitcast.10, bf16[128,512]{1,0:T(8,128)(2,1)} %start_codes.1, bf16[128,512]{1,0:T(8,128)(2,1)} %bitcast.11, bf16[128,512]{1,0:T(8,128)(2,1)} %loss_grads.1, bf16[512,512]{1,0:T(8,128)(2,1)} %bitcast.8, ...), custom_call_target="tpu_custom_call" | custom-call | tf_op jit(solution)/shard_map/pallas_call | solution.py:706
  92.0 0.0 copy-start
  92.0 1.6 %copy.14 = bf16[1,128,512]{2,1,0:T(8,128)(2,1)} copy(bf16[1,128,512]{2,1,0:T(8,128)(2,1)} %bitcast.15) | data formatting | bytes 262144
  93.6 0.0 copy-done
  93.6 0.7 copy.15
  (2 shorter events, 0.0 us)
Async XLA Ops:
  92.0 1.6 %copy-start = (bf16[128,512]{1,0:T(8,128)(2,1)S(1)}, bf16[128,512]{1,0:T(8,128)(2,1)}, u32[]{:S(2)}) copy-start(bf16[128,512]{1,0:T(8,128)(2,1)} %get-tuple-element.5) | copy-start | bytes 393220
